TPU v7x, 32 devices: a whole 2x2x4 slice. The times are simulated.
32 devices in a mesh: dp: 16 (over z, y, core), mp: 2 (over x).
Axes of the slice: x: 2, y: 2, z: 4, core: 2. Of those that a mesh axis runs over, the one named last changes fastest.
Arguments:
- inputs: bfloat16 [3, 1024, 2560], P(None, 'dp'), may hold values from -6 to 6
- gain_attn: float32 [2560], replicated, may hold values from 0.5 to 1.5
- w_query: bfloat16 [2560, 2560], P('dp', 'mp'), may hold values from -0.125 to 0.125
- w_keyval: bfloat16 [2560, 512], P('dp'), may hold values from -0.125 to 0.125
- w_output: bfloat16 [2560, 2560], P('mp', 'dp'), may hold values from -0.3125 to 0.3125
- gain_mlp: float32 [2560], replicated, may hold values from 0.5 to 1.5
- w_gate: bfloat16 [2560, 7680], P('dp', 'mp'), may hold values from -0.125 to 0.125
- b_gate: float32 [7680], P('mp'), may hold values from -3 to 3
- w_up: bfloat16 [2560, 7680], P('dp', 'mp'), may hold values from -0.125 to 0.125
- b_up: float32 [7680], P('mp'), may hold values from -3 to 3
- w_down: bfloat16 [7680, 2560], P('mp', 'dp'), may hold values from -0.125 to 0.125
- b_down: float32 [2560], replicated, may hold values from -3 to 3
- segment_ids: int32 [3, 16, 64], P(None, 'dp'), may hold values from 0 to 7, never falling along the last dimension, each value on 1 to 32 neighbouring positions
- cotangent: bfloat16 [3, 1024, 2560], P(None, 'dp'), may hold values from -12 to 12
Outputs:
- outputs: bfloat16 [3, 1024, 2560], P(None, 'dp')
- inputs_grad: bfloat16 [3, 1024, 2560], P(None, 'dp')
- gain_attn_grad: float32 [2560], replicated
- w_query_grad: float32 [2560, 2560], P('dp', 'mp')
- w_keyval_grad: float32 [2560, 512], P('dp')
- w_output_grad: float32 [2560, 2560], P('mp', 'dp')
- gain_mlp_grad: float32 [2560], replicated
- w_gate_grad: float32 [2560, 7680], P('dp', 'mp')
- b_gate_grad: float32 [7680], P('mp')
- w_up_grad: float32 [2560, 7680], P('dp', 'mp')
- b_up_grad: float32 [7680], P('mp')
- w_down_grad: float32 [7680, 2560], P('mp', 'dp')
- b_down_grad: float32 [2560], replicated
Inputs may be any that keep to these rules, and one draw needn't show every extreme that they name: `segment_ids`: ids never fall within a block of 64 tokens; a sequence holds 1 to 32 tokens and some sequence holds 32.
All inputs are finite; a program needn't handle non-finite values.
Results may differ from a plain program's by a relative error of at most 0.014.
Values may be sent and summed in bfloat16 or wider, within the bound.
No kernel may reach another device: no remote copies, remote signals or barrier semaphores. Data moves between devices by JAX's collectives and lax.ppermute only.
A program may use at most 384 MiB of HBM per device.

v0:
```python
import math
from functools import partial

import jax
import jax.numpy as jnp
from jax import lax
from jax.experimental import pallas as pl
from jax.experimental.pallas import tpu as pltpu
from jax.sharding import PartitionSpec as P

EPS = 1e-06
F32 = jnp.float32
BF16 = jnp.bfloat16
VMEM = 24 * 2**20
SCALE = 12.0
GELU_A, GELU_B = math.sqrt(2.0 / math.pi), 0.044715


def positions(segment):
    count = segment.shape[0]
    index = jnp.arange(count, dtype=jnp.int32)
    fresh = jnp.concatenate([jnp.ones((1,), jnp.bool_), segment[1:] != segment[:-1]])
    starts = lax.cummax(jnp.where(fresh, index, 0), axis=0)
    return (index - starts).astype(F32)


def inv_root(values):
    return lax.rsqrt(jnp.mean(values * values, axis=-1, keepdims=True) + EPS)


def norm_back(values, factor, gain, grad_norm):
    scaled = gain * grad_norm
    return factor * scaled - values * factor**3 * jnp.mean(scaled * values, axis=-1, keepdims=True)


def mm(left, right):
    return jnp.dot(left, right, preferred_element_type=F32)


def mm_nt(left, right):
    return lax.dot_general(left, right, (((1,), (1,)), ((), ())), preferred_element_type=F32)


def mm_tn(left, right):
    return lax.dot_general(left, right, (((0,), (0,)), ((), ())), preferred_element_type=F32)


class Grid:
    def __init__(self, total):
        self.z_count = total // 4
        spots = [(z, y, c) for z in range(self.z_count) for y in range(2) for c in range(2)]
        at = lambda z, y, c: (z * 2 + y) * 2 + c
        self.swap_y = [(at(z, y, c), at(z, 1 - y, c)) for z, y, c in spots]
        self.swap_c = [(at(z, y, c), at(z, y, 1 - c)) for z, y, c in spots]
        self.ring = lambda step: [
            (at(z, y, c), at((z + step) % self.z_count, y, c)) for z, y, c in spots
        ]
        self.flips = []
        step = 1
        while step < self.z_count:
            self.flips.append([(at(z, y, c), at(z ^ step, y, c)) for z, y, c in spots])
            step *= 2
        self.lines = [
            [at(z, y, c) for z in range(self.z_count)] for y in range(2) for c in range(2)
        ]
        index = lax.axis_index("dp")
        self.c = index % 2
        self.y = (index // 2) % 2
        self.z = index // 4
        self.x = lax.axis_index("mp")
        self.token = jnp.zeros((), F32)

    def wait(self, *values):
        self.token = lax.optimization_barrier((self.token, values))[0]

    def gate(self, value):
        return lax.optimization_barrier((value, self.token))[0]

    def over_y(self, value):
        return lax.ppermute(self.gate(value), "dp", self.swap_y)

    def over_c(self, value):
        return lax.ppermute(self.gate(value), "dp", self.swap_c)

    def over_x(self, value):
        return lax.ppermute(self.gate(value), "mp", [(0, 1), (1, 0)])

    def next_z(self, value, step=1):
        return lax.ppermute(self.gate(value), "dp", self.ring(step))

    def along_z(self, value):
        value = self.gate(value)
        return lax.all_to_all(value, "dp", 0, 0, axis_index_groups=self.lines, tiled=True)

    def behind(self, step):
        return lax.rem(self.z - step + 2 * self.z_count, self.z_count)


def pair(index, mine, other, axis):
    return jnp.where(
        index == 0, jnp.stack([mine, other], axis=axis), jnp.stack([other, mine], axis=axis)
    )


def take(value, index, axis):
    return lax.dynamic_index_in_dim(value, index, axis, keepdims=False)


def cost(micros):
    micros = micros / SCALE
    flops, moved = int(micros * 1.15e9), int(micros * 3.69e6)
    return pl.CostEstimate(flops=flops, bytes_accessed=moved, transcendentals=0)


def call(body, micros, grid, in_specs, outs, out_specs, operands, aliases=None, limit=VMEM):
    return pl.pallas_call(
        body,
        out_shape=[jax.ShapeDtypeStruct(shape, dtype) for shape, dtype in outs],
        grid_spec=pltpu.PrefetchScalarGridSpec(
            num_scalar_prefetch=1,
            grid=grid,
            in_specs=in_specs,
            out_specs=out_specs,
        ),
        input_output_aliases=aliases or {},
        cost_estimate=cost(micros),
        compiler_params=pltpu.CompilerParams(vmem_limit_bytes=limit),
    )(*operands)


def place_slot(ranks, pieces, wholes, z_count, cuts):
    rows, width = pieces[0].shape
    ends = list(cuts[1:]) + [width]
    given = len(wholes)

    def body(ranks_ref, *refs):
        sources, targets = refs[:4], refs[4 + given :]
        y, c = ranks_ref[1], ranks_ref[2]
        spots = [(y, c), (1 - y, c), (y, 1 - c), (1 - y, 1 - c)]
        for source, (at_y, at_c) in zip(sources, spots):
            for target, begin, end in zip(targets, cuts, ends):
                target[0, at_y, at_c] = source[:, begin:end]

    whole_spec = pl.BlockSpec(memory_space=pl.ANY)
    return call(
        body,
        1.0,
        (1,),
        [pl.BlockSpec((rows, width), lambda i, ranks: (0, 0))] * 4 + [whole_spec] * given,
        [((z_count, 2, 2, rows, end - begin), BF16) for begin, end in zip(cuts, ends)],
        [
            pl.BlockSpec((1, 2, 2, rows, end - begin), lambda i, ranks: (ranks[0], 0, 0, 0, 0))
            for begin, end in zip(cuts, ends)
        ],
        (ranks, *pieces, *wholes),
        aliases={5 + number: number for number in range(given)},
        limit=2 * VMEM,
    )


def place_all(ranks, pieces):
    z_count, rows, width = pieces[0].shape

    def body(ranks_ref, own, side, core, both, target):
        y, c = ranks_ref[1], ranks_ref[2]
        target[0, y, c] = own[0]
        target[0, 1 - y, c] = side[0]
        target[0, y, 1 - c] = core[0]
        target[0, 1 - y, 1 - c] = both[0]

    whole = call(
        body,
        1.0,
        (z_count,),
        [pl.BlockSpec((1, rows, width), lambda i, ranks: (i, 0, 0))] * 4,
        [((z_count, 2, 2, rows, width), BF16)],
        [pl.BlockSpec((1, 2, 2, rows, width), lambda i, ranks: (i, 0, 0, 0, 0))],
        (ranks, *pieces),
    )[0]
    return whole.reshape(z_count * 4 * rows, width)


def product(left, right, dtype):
    rows, depth = left.shape
    width = right.shape[1]
    block = 256 if width % 256 == 0 else width

    def body(ranks_ref, left_ref, right_ref, out_ref):
        out_ref[...] = mm(left_ref[...], right_ref[...]).astype(dtype)

    return call(
        body,
        1.0,
        (width // block,),
        [
            pl.BlockSpec((rows, depth), lambda i, ranks: (0, 0)),
            pl.BlockSpec((depth, block), lambda i, ranks: (0, i)),
        ],
        [((rows, width), dtype)],
        [pl.BlockSpec((rows, block), lambda i, ranks: (0, i))],
        (jnp.zeros((1,), jnp.int32), left, right),
    )[0]


def product_nt(ranks, left, right, groups):
    rows, depth = left.shape
    width = right.shape[0]
    block = 512 if width % 512 == 0 else width
    half = rows // groups // 2

    def body(ranks_ref, left_ref, right_ref, own_ref, other_ref):
        whole = mm_nt(left_ref[...], right_ref[...])
        low = ranks_ref[3] == 0
        for group in range(groups):
            at = group * 2 * half
            first, second = whole[at : at + half], whole[at + half : at + 2 * half]
            to = pl.ds(group * half, half)
            own_ref[to, :] = jnp.where(low, first, second)
            other_ref[to, :] = jnp.where(low, second, first).astype(BF16)

    out_spec = pl.BlockSpec((rows // 2, block), lambda i, ranks: (0, i))
    return call(
        body,
        1.0,
        (width // block,),
        [
            pl.BlockSpec((rows, depth), lambda i, ranks: (0, 0)),
            pl.BlockSpec((block, depth), lambda i, ranks: (i, 0)),
        ],
        [((rows // 2, width), F32), ((rows // 2, width), BF16)],
        [out_spec] * 2,
        (ranks, left, right),
    )


def second_norm(x_ref, mine_ref, got_ref, gain_ref, residual_ref, factor_ref, normed_ref):
    residual = x_ref[...].astype(F32) + mine_ref[...] + got_ref[...].astype(F32)
    factor = inv_root(residual)
    residual_ref[...], factor_ref[...] = residual, factor
    normed_ref[...] = (residual * factor * gain_ref[...]).astype(BF16)


def second_norm_back(
    own_ref, got_ref, held_ref, residual_ref, factor_ref, gain_ref, bias_ref, dy_ref,
    grad_ref, grad_b_ref, term_ref, out_ref,
):
    both = [
        own_ref[at].astype(F32) + got_ref[at].astype(F32) + held_ref[at].astype(F32) for at in (0, 1)
    ]
    residual, factor = residual_ref[...], factor_ref[...]
    out_ref[...] = (residual + both[1] + bias_ref[...]).astype(BF16)
    term_ref[...] = jnp.sum(both[0] * residual * factor, axis=0, keepdims=True)
    grad = dy_ref[...].astype(F32) + norm_back(residual, factor, gain_ref[...], both[0])
    grad_ref[...], grad_b_ref[...] = grad, grad.astype(BF16)


def first_norm_back(mine_ref, got_ref, x_ref, factor_ref, gain_ref, grad_ref, out_ref, term_ref):
    grad = mine_ref[...] + got_ref[...].astype(F32)
    values, factor = x_ref[...].astype(F32), factor_ref[...]
    term_ref[...] = jnp.sum(grad * values * factor, axis=0, keepdims=True)
    out_ref[...] = (grad_ref[...] + norm_back(values, factor, gain_ref[...], grad)).astype(BF16)


def product_rows(ranks, lefts, groups, z_count, cuts=1, beside=False):
    features = lefts[0].shape[1]
    width = sum(right.shape[1] for right in groups[0]) if beside else groups[0][0].shape[1]
    rows = features // (4 * z_count)
    block = math.lcm(4 * rows, 128)
    span = block // (4 * rows)
    rights = [right for group in groups for right in group]
    each = len(groups[0])
    join = lambda parts: parts[0] if len(parts) == 1 else jnp.concatenate(parts, axis=0)

    def body(ranks_ref, *refs):
        left = [ref[...] for ref in refs[: len(lefts)]]
        left = left if beside else join(left)
        right_refs, out_refs = refs[len(lefts) : -outs], refs[-outs:]
        low = ranks_ref[2] == 0
        here = pl.program_id(0)
        for number in range(len(groups)):
            right = [ref[...] for ref in right_refs[number * each : (number + 1) * each]]
            keep, sends = out_refs[number], out_refs[len(groups) + number * cuts * z_count :]
            if beside:
                whole = jnp.concatenate([mm_tn(a, b) for a, b in zip(left, right)], axis=1)
            else:
                whole = mm_tn(left, join(right))
            for place in range(span):
                for y in range(2):
                    at = (place * 4 + y * 2) * rows
                    first, second = whole[at : at + rows], whole[at + rows : at + 2 * rows]
                    keep[place, y] = jnp.where(low, first, second).astype(BF16)
                    other = jnp.where(low, second, first).astype(BF16)
                    for z in range(place, z_count, span):

                        @pl.when(here == z // span)
                        def _(target=sends[cuts * z + (y if cuts == 2 else 0)], y=y, other=other):
                            target[y % (2 // cuts)] = other

    parts = cuts * z_count
    outs = len(groups) * (1 + parts)
    keep_spec = pl.BlockSpec((span, 2, rows, width), lambda i, ranks: (i, 0, 0, 0))
    send_spec = pl.BlockSpec((2 // cuts, rows, width), lambda i, ranks: (0, 0, 0))
    out = call(
        body,
        2.0 * len(groups),
        (features // block,),
        [pl.BlockSpec((left.shape[0], block), lambda i, ranks: (0, i)) for left in lefts]
        + [pl.BlockSpec(right.shape, lambda i, ranks: (0, 0)) for right in rights],
        [((z_count, 2, rows, width), BF16)] * len(groups)
        + [((2 // cuts, rows, width), BF16)] * (len(groups) * parts),
        [keep_spec] * len(groups) + [send_spec] * (len(groups) * parts),
        (ranks, *lefts, *rights),
    )
    sends = out[len(groups) :]
    return [
        (out[number], sends[number * parts : (number + 1) * parts])
        for number in range(len(groups))
    ]


def mlp_slot(wg, wu, wd, bg, bu, own, other, dy_own, dy_other):
    features, hidden = wg.shape
    half = own.shape[0]
    block = features // 4 if (features // 4) % 128 == 0 else features

    def body(
        wg_ref, wu_ref, wd_ref, bg_ref, bu_ref, own_ref, other_ref, dyo_ref, dyr_ref,
        hid_ref, dg_ref, du_ref, own_back, other_back, sum_ref, b_all, dy_all,
    ):
        b_all[:half], b_all[half:] = own_ref[...], other_ref[...]
        dy_all[:half], dy_all[half:] = dyo_ref[...], dyr_ref[...]
        gate = mm(b_all[...], wg_ref[...]) + bg_ref[...]
        up = mm(b_all[...], wu_ref[...]) + bu_ref[...]
        grad_inner = mm(dy_all[...], wd_ref[...])
        bend = jnp.tanh(GELU_A * (gate + GELU_B * gate * gate * gate))
        gelu = 0.5 * gate * (1.0 + bend)
        slope = 0.5 * (1.0 + bend) + 0.5 * gate * (1.0 - bend * bend) * (
            GELU_A * (1.0 + 3.0 * GELU_B * gate * gate)
        )
        hid_ref[...] = (gelu * up).astype(BF16)
        for row, target, value in (
            (0, dg_ref, grad_inner * up * slope),
            (1, du_ref, grad_inner * gelu),
        ):
            value = value.astype(BF16)
            target[...] = value
            sum_ref[row : row + 1] = jnp.sum(value.astype(F32), axis=0, keepdims=True)
        for step in range(features // block):
            at = pl.ds(step * block, block)
            part = mm_nt(dg_ref[...], wg_ref[at, :]) + mm_nt(du_ref[...], wu_ref[at, :])
            own_back[0, :, at], other_back[0, :, at] = part[:half].astype(BF16), part[half:].astype(BF16)
            part = mm_nt(hid_ref[...], wd_ref[at, :])
            own_back[1, :, at], other_back[1, :, at] = part[:half].astype(BF16), part[half:].astype(BF16)

    weights = [pltpu.with_memory_space_constraint(w, pltpu.VMEM) for w in (wg, wu, wd)]
    return in_vmem(
        body,
        4.0,
        [((2 * half, hidden), BF16)] * 3
        + [((2, half, features), BF16)] * 2
        + [((2, hidden), F32)],
        *(*weights, bg[None], bu[None], own, other, dy_own, dy_other),
        scratch=[pltpu.VMEM((2 * half, features), BF16)] * 2,
    )


def split_columns(grid, shard):
    rows, width = shard.shape
    return shard.reshape(rows, grid.z_count, width // grid.z_count).transpose(1, 0, 2)


def pick(values, index):
    chosen = values[0]
    for number in range(1, len(values)):
        chosen = jnp.where(index == number, values[number], chosen)
    return chosen


def own_rows(ranks, keep, got, parts=1):
    z_count, _, rows, width = keep.shape
    cuts, each = len(got) // z_count, z_count // parts

    def body(ranks_ref, keep_ref, *refs):
        y = ranks_ref[1]
        for z in range(z_count):

            @pl.when(pl.program_id(0) == z)
            def _(got_refs=refs[cuts * z : cuts * z + cuts], away=refs[cuts * z_count + z // each]):
                halves = [got_refs[at % cuts][at // cuts] for at in (0, 1)]
                sums = [keep_ref[0, at].astype(F32) + halves[at].astype(F32) for at in (0, 1)]
                away[0] = jnp.where(y == 0, sums[1], sums[0]).astype(BF16)
                refs[-1][0] = jnp.where(y == 0, sums[0], sums[1]).astype(BF16)

    block = pl.BlockSpec((1, 2, rows, width), lambda i, ranks: (i, 0, 0, 0))
    whole = pl.BlockSpec((2 // cuts, rows, width), lambda i, ranks: (0, 0, 0))
    outs = [((each, rows, width), BF16)] * parts + [((z_count, rows, width), BF16)]
    half = pl.BlockSpec((1, rows, width), lambda i, ranks: (i, 0, 0))
    specs = [block] + [whole] * (cuts * z_count)
    out_specs = [part_spec(rows, width, part, each) for part in range(parts)] + [half]
    out = call(body, 0.5, (z_count,), specs, outs, out_specs, (ranks, keep, *got))
    return (out[0] if parts == 1 else out[:-1]), out[-1]


def part_spec(rows, width, part, each):
    return pl.BlockSpec(
        (1, rows, width), lambda i, ranks: (jnp.clip(i - part * each, 0, each - 1), 0, 0)
    )


def plus(left, *rights):
    z_count, rows, width = left.shape
    each = z_count // len(rights)

    def body(ranks_ref, left_ref, *refs):
        for part, right_ref in enumerate(refs[:-1]):

            @pl.when(pl.program_id(0) // each == part)
            def _(right_ref=right_ref):
                refs[-1][...] = (left_ref[...].astype(F32) + right_ref[...].astype(F32)).astype(BF16)

    block = pl.BlockSpec((1, rows, width), lambda i, ranks: (i, 0, 0))
    specs = [block] + [part_spec(rows, width, part, each) for part in range(len(rights))]
    operands = (jnp.zeros((1,), jnp.int32), left, *rights)
    return call(body, 0.5, (z_count,), specs, [(left.shape, BF16)], [block], operands)[0]


def ring_sum(grid, parts, held, step):
    _, rows, width = parts.shape
    dtype = BF16 if step < grid.z_count else F32
    given = [] if held is None else [held]

    def body(ranks_ref, part_ref, *refs):
        part = part_ref[0].astype(F32)
        refs[-1][...] = (part + refs[0][...].astype(F32) if given else part).astype(dtype)

    full = pl.BlockSpec((rows, width), lambda i, ranks: (0, 0))
    spot = grid.behind(step).astype(jnp.int32)[None]
    return call(
        body,
        1.0,
        (1,),
        [pl.BlockSpec((1, rows, width), lambda i, ranks: (ranks[0], 0, 0))] + [full] * len(given),
        [((rows, width), dtype)],
        [full],
        (spot, parts, *given),
    )[0]


def add(*values):
    def body(*refs):
        total = refs[0][...].astype(F32)
        for ref in refs[1:-1]:
            total += ref[...].astype(F32)
        refs[-1][...] = total.astype(BF16)

    values = [value for value in values if value is not None]
    return in_vmem(body, 1.0, [(values[0].shape, BF16)], *values)[0]


def collect_columns(parts, turn=False):
    count, rows, width = parts.shape

    def body(parts_ref, out_ref):
        if turn:
            for step in range(count):
                out_ref[step * width : (step + 1) * width, :] = parts_ref[step].astype(F32).T
        else:
            pieces = [parts_ref[step].astype(F32) for step in range(count)]
            out_ref[...] = jnp.concatenate(pieces, axis=1)

    shape = (count * width, rows) if turn else (rows, count * width)
    return in_vmem(body, 3.0, [(shape, F32)], parts)[0]


def turned(value, cosine, sine):
    first = value[:, : cosine.shape[1]]
    first = first * cosine + pltpu.roll(first, first.shape[1] // 2, 1) * sine
    return jnp.concatenate([first, value[:, cosine.shape[1] :]], axis=1)


def softmax(query, key, bias):
    scores = mm_nt(query, key) + bias
    expon = jnp.exp(scores - jnp.max(scores, axis=-1, keepdims=True))
    return expon / jnp.sum(expon, axis=-1, keepdims=True)


def attend(scale, q_ref, k_ref, v_ref, cos_ref, sin_ref, bias_ref, rq_ref, o_ref):
    size = k_ref.shape[1]
    for head in range(rq_ref.shape[1] // size):
        at = pl.ds(head * size, size)
        query = (turned(q_ref[:, at], cos_ref[...], sin_ref[...]) * scale).astype(BF16)
        rq_ref[:, at] = query
        probs = softmax(query, k_ref[...], bias_ref[...]).astype(BF16)
        o_ref[:, at] = mm(probs, v_ref[...]).astype(BF16)


def attend_back(
    scale, do_ref, rq_ref, k_ref, v_ref, cos_ref, sin_ref, bias_ref, dq_ref, dk_ref, dv_ref
):
    size = k_ref.shape[1]
    cosine, sine = cos_ref[...], -sin_ref[...]
    grad_key = jnp.zeros(dk_ref.shape, F32)
    grad_value = jnp.zeros(dv_ref.shape, F32)
    for head in range(rq_ref.shape[1] // size):
        at = pl.ds(head * size, size)
        query, grad_out = rq_ref[:, at], do_ref[:, at]
        probs = softmax(query, k_ref[...], bias_ref[...])
        grad_value += mm_tn(probs.astype(BF16), grad_out)
        grad_probs = mm_nt(grad_out, v_ref[...])
        delta = jnp.sum(probs * grad_probs, axis=-1, keepdims=True)
        grad_scores = (probs * (grad_probs - delta)).astype(BF16)
        grad_query = mm(grad_scores, k_ref[...]) * scale
        dq_ref[:, at] = turned(grad_query, cosine, sine).astype(BF16)
        grad_key += mm_tn(grad_scores, query)
    dk_ref[...] = turned(grad_key, cosine, sine)
    dv_ref[...] = grad_value


def in_vmem(body, micros, shapes, *operands, scratch=()):
    spec = pl.BlockSpec(memory_space=pltpu.VMEM)
    return pl.pallas_call(
        body,
        out_shape=[jax.ShapeDtypeStruct(shape, dtype) for shape, dtype in shapes],
        in_specs=[spec] * len(operands),
        out_specs=[spec] * len(shapes),
        scratch_shapes=list(scratch),
        cost_estimate=cost(micros),
        compiler_params=pltpu.CompilerParams(vmem_limit_bytes=VMEM),
    )(*operands)


def shards(
    inputs,
    gain_attn,
    w_query,
    w_keyval,
    w_output,
    gain_mlp,
    w_gate,
    b_gate,
    w_up,
    b_up,
    w_down,
    b_down,
    segment_ids,
    cotangent,
    total,
):
    grid = Grid(total)
    count = grid.z_count
    micro, length, width = inputs.shape
    tokens = micro * length
    head_dim = w_keyval.shape[1] // 2
    query_width = w_query.shape[1]
    scale = head_dim ** (-0.5)

    def halves(value):
        value = value.reshape(micro, 2, length // 2, value.shape[-1])
        return tuple(take(value, i, 1).reshape(tokens // 2, -1) for i in (grid.x, 1 - grid.x))

    def join(mine, other):
        shape = (micro, length // 2, mine.shape[-1])
        return pair(grid.x, mine.reshape(shape), other.reshape(shape), 1).reshape(tokens, -1)

    ranks = jnp.stack([grid.z, grid.y, grid.c, grid.x]).astype(jnp.int32)
    keyval_half = lax.dynamic_slice_in_dim(w_keyval, grid.x * head_dim, head_dim, 1)
    shards_of = [split_columns(grid, shard) for shard in (w_gate, w_up, w_down.T)]
    dy_half = halves(cotangent.reshape(tokens, width))[0]
    segment = segment_ids.reshape(micro, length)
    offsets = jax.vmap(positions)(segment).reshape(tokens)
    quarter = head_dim // 4
    freqs = 10000.0 ** (-jnp.arange(quarter, dtype=F32) / quarter)
    angle = offsets[:, None] * freqs[None, :]
    cosine, sine = jnp.cos(angle), jnp.sin(angle)
    cosine = jnp.concatenate([cosine, cosine], axis=1)
    sine = jnp.concatenate([-sine, sine], axis=1)
    index = jnp.arange(tokens, dtype=jnp.int32)
    seg = segment.reshape(tokens)
    allowed = (
        (seg[:, None] == seg[None, :])
        & (index[:, None] // length == index[None, :] // length)
        & (index[None, :] <= index[:, None])
    )
    bias = jnp.where(allowed, 0.0, -1e30).astype(F32)
    hidden_x = inputs.reshape(tokens, width).astype(F32)
    factor_one = inv_root(hidden_x)
    normed = (hidden_x * factor_one * gain_attn).astype(BF16)
    x_half, factor_half = halves(inputs.reshape(tokens, width))[0], halves(factor_one)[0]
    half_shape = (tokens // 2, width)

    def mlp(step):
        pieces = (b_slots[step], b_others[step], dy_slots[step], dy_others[step])
        results.append(mlp_slot(wg, wu, wd, bg, bu, *grid.gate(pieces)))
        grid.wait(*results[-1])

    slots = [jnp.concatenate([w_query, keyval_half, w_output.T], axis=1)]
    across, beside, both, wholes = [], [], [], []
    dy_slots, dy_others = [dy_half], []

    def place(step):
        pieces = [slots[step], across[step], beside[step], both[step]]
        spot = jnp.stack([grid.behind(step), grid.y, grid.c]).astype(jnp.int32)
        return place_slot(spot, pieces, wholes, count, (0, query_width + head_dim))

    for step in range(count):
        if step + 1 < count:
            slots.append(grid.next_z(slots[step]))
        else:
            gate_mine = grid.along_z(shards_of[0])
        across.append(grid.over_y(slots[step]))
        beside.append(grid.over_c(slots[step]))
        if step == 0:
            dy_others.append(grid.over_x(dy_half))
            grid.wait(shards_of[0])
        else:
            both.append(grid.over_c(across[step - 1]))
            wholes = place(step - 1)
            grid.wait(*wholes, beside[step])
        if step == 1:
            grid.wait(shards_of[1], normed, x_half, dy_others[0])
        if step == 2:
            grid.wait(shards_of[2], cosine, sine, bias)
        if step + 1 < count:
            grid.wait(slots[step + 1], across[step])
    grid.wait(across[-1])
    both.append(grid.over_c(across[-1]))
    grid.wait(gate_mine)

    up_mine = grid.along_z(shards_of[1])
    gate_across, gate_beside = grid.over_y(gate_mine), grid.over_c(gate_mine)
    wholes = place(count - 1)
    w_qkv, w_out = [whole.reshape(width, -1) for whole in wholes]
    queries = product(normed, w_qkv, F32)
    keyval = queries[:, query_width:]
    front, back = keyval[:, :quarter], keyval[:, quarter : 2 * quarter]
    swapped = jnp.concatenate([back, front], axis=1)
    key = jnp.concatenate(
        [keyval[:, : 2 * quarter] * cosine + swapped * sine, keyval[:, 2 * quarter :]], axis=1
    )
    keyval = jnp.where(grid.x == 0, key, keyval).astype(BF16)
    keyval_other = grid.over_x(keyval)
    grid.wait(keyval_other)
    rot_key = jnp.where(grid.x == 0, keyval, keyval_other)
    values_in = jnp.where(grid.x == 0, keyval_other, keyval)
    shape = (tokens, query_width)
    rot_query, mixed_b = in_vmem(
        partial(attend, scale),
        1.2,
        [(shape, BF16), (shape, BF16)],
        *(queries, rot_key, values_in, cosine, sine, bias),
    )
    mine, other = product_nt(ranks, mixed_b, w_out, micro)
    grid.wait(mine)
    attended = grid.over_x(other)
    grid.wait(up_mine)
    down_mine = grid.along_z(shards_of[2])
    grid.wait(gate_across)
    up_across, up_beside = grid.over_y(up_mine), grid.over_c(up_mine)
    gate_both = grid.over_c(gate_across)
    grid.wait(attended)
    residual, factor_two, normed_two = in_vmem(
        second_norm,
        0.5,
        [(half_shape, F32), ((tokens // 2, 1), F32), (half_shape, BF16)],
        *(x_half, mine, attended, gain_mlp[None]),
    )
    grid.wait(normed_two)
    b_slots, b_others = [normed_two], [grid.over_x(normed_two)]
    b_slots.append(grid.next_z(normed_two))
    dy_slots.append(grid.next_z(dy_half))
    wg = place_all(ranks, [gate_mine, gate_across, gate_beside, gate_both])
    grid.wait(wg, b_others[0])
    grid.wait(down_mine)

    grid.wait(up_across)
    down_across, down_beside = grid.over_y(down_mine), grid.over_c(down_mine)
    grid.wait(b_slots[1], dy_slots[1])
    for step in range(1, count - 1):
        b_slots.append(grid.next_z(b_slots[step]))
        dy_slots.append(grid.next_z(dy_slots[step]))
        b_others.append(grid.over_x(b_slots[step]))
        dy_others.append(grid.over_x(dy_slots[step]))
        if step == 1:
            up_both = grid.over_c(up_across)
            wu = place_all(ranks, [up_mine, up_across, up_beside, up_both])
            grid.wait(wu)
        if step == 2:
            grid.wait(down_across)
            down_both = grid.over_c(down_across)
            wd = place_all(ranks, [down_mine, down_across, down_beside, down_both])
            hidden = wg.shape[1]
            spot = grid.z * hidden
            bg = lax.dynamic_slice_in_dim(b_gate, spot, hidden, 0)
            bu = lax.dynamic_slice_in_dim(b_up, spot, hidden, 0)
            grid.wait(wd, bg, bu)
            results = []
            mlp(0)
        grid.wait(b_slots[step + 1], dy_slots[step + 1])
        grid.wait(b_others[step], dy_others[step])
    b_others.append(grid.over_x(b_slots[-1]))
    dy_others.append(grid.over_x(dy_slots[-1]))
    mlp(1)

    for step in range(2, count - 1):
        mlp(step)
    grid.wait(b_others[-1], dy_others[-1])
    back_got = [None, grid.over_x(results[1][4])]
    mlp(count - 1)
    inner_slots, gate_slots, up_slots, back_own, back_other, sums = zip(*results)
    dy_all = [piece for two in zip(dy_slots, dy_others) for piece in two]
    b_all = [piece for two in zip(b_slots, b_others) for piece in two]
    down_keep, down_send = product_rows(ranks, grid.gate(dy_all), [inner_slots], count, 2)[0]
    grid.wait(down_keep, back_got[1])
    held = add(back_own[1], back_got[1])
    grid.wait(held)
    back_next = grid.next_z(held)
    back_got.append(grid.over_x(back_other[2]))
    down_got = [grid.over_c(send) for send in down_send]
    grid.wait(*down_got)
    down_away, down_stay = own_rows(ranks, grid.gate(down_keep), down_got)
    grid.wait(down_away)
    down_back = grid.over_y(down_away)
    (gate_keep, gate_send), (up_keep, up_send) = product_rows(
        ranks, grid.gate(b_all), [gate_slots, up_slots], count
    )
    grid.wait(gate_keep, back_got[2], back_next)
    held = add(back_own[2], back_got[2], back_next)
    grid.wait(held)
    back_next = grid.next_z(held)
    back_got.append(grid.over_x(back_other[3]))
    gate_got = [grid.over_c(send) for send in gate_send]
    grid.wait(*gate_got)
    gate_away, gate_stay = own_rows(ranks, grid.gate(gate_keep), gate_got)
    grid.wait(gate_away)
    for step in range(3, count):
        grid.wait(back_got[step], back_next)
        held = add(back_own[step], back_got[step], back_next)
        grid.wait(held)
        back_next = grid.next_z(held)
        back_got.append(grid.over_x(back_other[(step + 1) % count]))
    up_got = [grid.over_c(send) for send in up_send]
    grid.wait(down_back)
    gate_back = grid.over_y(gate_away)
    down_rows = plus(grid.gate(down_stay), down_back)
    grid.wait(down_rows)
    down_parts = grid.along_z(down_rows)
    grid.wait(*up_got)
    up_away, up_stay = own_rows(ranks, grid.gate(up_keep), up_got, 2)
    grid.wait(*up_away)
    grid.wait(back_got[-1], back_next)
    grad_resid, grad_resid_b, gain_mlp_term, outputs = in_vmem(
        second_norm_back,
        0.5,
        [(half_shape, F32), (half_shape, BF16), ((1, width), F32), (half_shape, BF16)],
        *(back_own[0], back_got[-1], back_next, residual, factor_two),
        *(gain_mlp[None], b_down[None], dy_half),
    )
    grid.wait(grad_resid_b)
    grad_resid_other = grid.over_x(grad_resid_b)
    grid.wait(gate_back)
    up_back = [grid.over_y(up_away[0])]
    gate_rows = plus(grid.gate(gate_stay), gate_back)
    grid.wait(gate_rows, grad_resid_other)

    grad_resid_b = join(grad_resid_b, grad_resid_other)
    grad_mixed = product(grid.gate(grad_resid_b), w_out, BF16)
    shape_kv = (tokens, head_dim)
    grad_query, grad_key, grad_values = in_vmem(
        partial(attend_back, scale),
        0.5,
        [(shape, BF16), (shape_kv, F32), (shape_kv, F32)],
        *(grad_mixed, rot_query, rot_key, values_in, cosine, sine, bias),
    )
    grid.wait(grad_query)
    grad_own = jnp.where(grid.x == 0, grad_key, grad_values)
    grad_other = grid.over_x(jnp.where(grid.x == 0, grad_values, grad_key))
    grid.wait(up_back[0])
    up_back.append(grid.over_y(up_away[1]))
    query_keep, query_send = product_rows(ranks, [grid.gate(normed)], [[grad_query]], count)[0]
    grid.wait(grad_other, query_keep, up_back[1])
    grid.wait(down_parts)
    gate_parts = grid.along_z(gate_rows)
    up_rows = plus(grid.gate(up_stay), *up_back)
    grid.wait(up_rows)
    grad_keyval = (grad_own + grad_other).astype(BF16)
    out_keep, out_send = product_rows(
        ranks, [grid.gate(grad_resid_b), normed], [[mixed_b, grad_keyval]], count, beside=True
    )[0]
    grid.wait(out_keep)
    out_got = [grid.over_c(send) for send in out_send]
    grid.wait(*out_got)
    out_away, out_stay = own_rows(ranks, grid.gate(out_keep), out_got, 2)
    grid.wait(*out_away)
    out_back = [grid.over_y(out_away[0])]
    grid.wait(gate_parts)
    up_parts = grid.along_z(up_rows)
    mine, other = product_nt(
        ranks, jnp.concatenate([grad_query, grid.gate(grad_keyval)], axis=1), w_qkv, micro
    )
    grid.wait(mine)
    grad_normed = grid.over_x(other)
    query_got = [grid.over_c(send) for send in query_send]
    grid.wait(out_back[0])
    out_back.append(grid.over_y(out_away[1]))
    grid.wait(*query_got)
    query_away, query_stay = own_rows(ranks, grid.gate(query_keep), query_got)
    grid.wait(query_away)
    grid.wait(grad_normed)
    grad_input, gain_attn_term = in_vmem(
        first_norm_back,
        0.5,
        [(half_shape, BF16), ((1, width), F32)],
        *(mine, grad_normed, x_half, factor_half, gain_attn[None], grid.gate(grad_resid)),
    )
    grid.wait(grad_input)
    narrow = jnp.concatenate(
        [gain_attn_term, gain_mlp_term, jnp.sum(dy_half.astype(F32), axis=0)[None]]
    )
    grid.wait(narrow)
    narrow_other = grid.over_x(narrow)
    outputs_other = grid.over_x(outputs)
    down_grad = collect_columns(grid.gate(down_parts), True)
    grid.wait(down_grad)
    grid.wait(out_back[1])
    query_back = grid.over_y(query_away)
    out_rows = plus(grid.gate(out_stay), *out_back)
    out_held = ring_sum(grid, out_rows, None, 1)
    grid.wait(out_held)
    out_held = grid.next_z(out_held)

    ffn = b_gate.shape[0]
    wide = jnp.zeros((2, ffn), F32)
    wide = lax.dynamic_update_slice(wide, sum(sums), (0, spot)).reshape(-1)
    grid.wait(narrow_other)
    small = jnp.concatenate([(narrow + narrow_other).reshape(-1), wide])
    small_other = grid.over_c(small)
    grid.wait(small_other)
    small = small + small_other
    grid.wait(small)
    small_all = [small] + [grid.next_z(small, step) for step in range(1, count)]
    grid.wait(out_held)
    out_held = ring_sum(grid, out_rows, out_held, 2)
    grid.wait(out_held)
    out_held = grid.next_z(out_held)
    grid.wait(up_parts)
    gate_grad = collect_columns(grid.gate(gate_parts))
    grid.wait(gate_grad)
    grid.wait(query_back)
    query_rows = plus(grid.gate(query_stay), query_back)
    query_held = ring_sum(grid, query_rows, None, 1)
    grid.wait(query_held)
    query_held = grid.next_z(query_held)
    grid.wait(outputs_other, *small_all)
    places = [lax.rem(grid.z - z + count, count) for z in range(count)]
    small = sum(pick(small_all, place) for place in places)
    grid.wait(small)
    small_other = grid.over_y(small)
    grad_input_other = grid.over_x(grad_input)
    for step in range(3, count):
        grid.wait(out_held)
        out_held = ring_sum(grid, out_rows, out_held, step)
        grid.wait(out_held)
        out_held = grid.next_z(out_held)
    grid.wait(query_held)
    query_held = ring_sum(grid, query_rows, query_held, 2)
    grid.wait(query_held)
    query_held = grid.next_z(query_held)
    up_grad = collect_columns(grid.gate(up_parts))
    grid.wait(up_grad)
    grid.wait(out_held)
    out_held = ring_sum(grid, out_rows, out_held, count)
    grid.wait(out_held)
    keyval_grad = out_held[:, query_width:]
    keyval_other = grid.over_x(keyval_grad)
    out_grad = out_held[:, :query_width].T
    for step in range(3, count):
        grid.wait(query_held)
        query_held = ring_sum(grid, query_rows, query_held, step)
        grid.wait(query_held)
        query_held = grid.next_z(query_held)
    grid.wait(out_grad, keyval_other, grad_input_other)
    small = small + small_other
    query_grad = ring_sum(grid, query_rows, grid.gate(query_held), count)
    keyval_grad = pair(grid.x, keyval_grad, keyval_other, 1)
    keyval_grad = keyval_grad.reshape(keyval_grad.shape[0], 2 * head_dim)
    return (
        join(outputs, outputs_other).reshape(inputs.shape),
        join(grad_input, grad_input_other).reshape(inputs.shape),
        small[:width],
        query_grad,
        keyval_grad,
        out_grad,
        small[width : 2 * width],
        gate_grad,
        small[3 * width : 3 * width + ffn],
        up_grad,
        small[3 * width + ffn :],
        down_grad,
        small[2 * width : 3 * width],
    )


def solution(mesh):
    in_specs = (
        P(None, "dp", None),
        P(),
        P("dp", "mp"),
        P("dp", None),
        P("mp", "dp"),
        P(),
        P("dp", "mp"),
        P("mp"),
        P("dp", "mp"),
        P("mp"),
        P("mp", "dp"),
        P(),
        P(None, "dp", None),
        P(None, "dp", None),
    )
    out_specs = (
        P(None, "dp", None),
        P(None, "dp", None),
        P(),
        P("dp", "mp"),
        P("dp", None),
        P("mp", "dp"),
        P(),
        P("dp", "mp"),
        P("mp"),
        P("dp", "mp"),
        P("mp"),
        P("mp", "dp"),
        P(),
    )
    body = partial(shards, total=mesh.shape["dp"])
    return jax.shard_map(body, mesh=mesh, in_specs=in_specs, out_specs=out_specs, check_vma=False)
```

profile of v0, /device:TPU:0, one launch (start us, length us, event | category | flops | bytes accessed | tf_op | source)
XLA Modules:
  0.0 591.5 jit_solution(9220699043243360860)
XLA Ops:
  2.8 3.1 collective-permute-start
  10.0 2.8 copy.61
  15.4 12.5 %collective-permute-done.refs_0_ = bf16[160,2816]{1,0:T(8,128)(2,1)} collective-permute-done((bf16[160,2816]{1,0:T(8,128)(2,1)S(1)}, bf16[160,2816]{1,0:T(8,128)(2,1)}, u32[]{:S(2)}, u32[]{:S(2)}) %collective-permute-start) | collective-permute-done | bytes 901152 | tf_op jit(solution)/shard_map/ppermute | solution.py:89
  33.1 4.4 reshape.230
  40.4 4.4 reshape.233
  50.0 4.0 shard_map.237
  59.1 4.3 shard_map.238
  64.3 14.3 %collective-permute-done.10.refs_0_ = bf16[160,2816]{1,0:T(8,128)(2,1)} collective-permute-done((bf16[160,2816]{1,0:T(8,128)(2,1)}, bf16[160,2816]{1,0:T(8,128)(2,1)}, u32[]{:S(2)}, u32[]{:S(2)}) %collective-permute-start.10) | collective-permute-done | bytes 901152 | tf_op jit(solution)/shard_map/ppermute | solution.py:89
  78.7 3.5 all-to-all-start
  86.3 4.4 shard_map.239
  90.7 14.4 %collective-permute-done.14.refs_1_ = bf16[160,2816]{1,0:T(8,128)(2,1)} collective-permute-done((bf16[160,2816]{1,0:T(8,128)(2,1)}, bf16[160,2816]{1,0:T(8,128)(2,1)}, u32[]{:S(2)}, u32[]{:S(2)}) %collective-permute-start.14) | collective-permute-done | bytes 901152 | tf_op jit(solution)/shard_map/ppermute | solution.py:80
  105.1 8.3 %all-to-all-done.own = bf16[4,160,960]{2,1,0:T(8,128)(2,1)S(1)} async-done(((bf16[4,160,960]{2,1,0:T(8,128)(2,1)}), bf16[4,160,960]{2,1,0:T(8,128)(2,1)S(1)}, u32[]{:S(2)}, u32[]{:S(2)}) %all-to-all-start) | async-done | bytes 1228832 | tf_op jit(solution)/shard_map/all_to_all | solution.py:93
  113.5 4.3 all-to-all-start.1
  117.9 4.5 shard_map.240
  122.4 3.2 copy-done.2
  125.7 3.2 shard_map.241.q_ref
  131.0 3.4 collective-permute-done.18
  135.6 3.6 shard_map.243
  141.0 7.6 %all-to-all-done.1.own = bf16[4,160,960]{2,1,0:T(8,128)(2,1)} async-done(((bf16[4,160,960]{2,1,0:T(8,128)(2,1)}), bf16[4,160,960]{2,1,0:T(8,128)(2,1)}, u32[]{:S(2)}, u32[]{:S(2)}) %all-to-all-start.1) | async-done | bytes 1228832 | tf_op jit(solution)/shard_map/all_to_all | solution.py:93
  148.7 4.8 all-to-all-start.2
  153.5 5.4 collective-permute-done.15.side
  160.6 12.4 %collective-permute-done.22.got_ref = bf16[96,2560]{1,0:T(8,128)(2,1)S(1)} collective-permute-done((bf16[96,2560]{1,0:T(8,128)(2,1)}, bf16[96,2560]{1,0:T(8,128)(2,1)S(1)}, u32[]{:S(2)}, u32[]{:S(2)}) %collective-permute-start.22) | collective-permute-done | bytes 491552 | tf_op jit(solution)/shard_map/ppermute | solution.py:86
  180.6 2.8 shard_map.244
  185.8 3.4 collective-permute-done.23.other_ref.refs_1_
  189.1 16.2 %all-to-all-done.2.own = bf16[4,160,960]{2,1,0:T(8,128)(2,1)} async-done(((bf16[4,160,960]{2,1,0:T(8,128)(2,1)}), bf16[4,160,960]{2,1,0:T(8,128)(2,1)}, u32[]{:S(2)}, u32[]{:S(2)}) %all-to-all-start.2) | async-done | bytes 1228832 | tf_op jit(solution)/shard_map/all_to_all | solution.py:93
  208.2 14.1 %collective-permute-done.30.dyo_ref.refs_4_ = bf16[96,2560]{1,0:T(8,128)(2,1)} collective-permute-done((bf16[96,2560]{1,0:T(8,128)(2,1)}, bf16[96,2560]{1,0:T(8,128)(2,1)}, u32[]{:S(2)}, u32[]{:S(2)}) %collective-permute-start.30) | collective-permute-done | bytes 491552 | tf_op jit(solution)/shard_map/ppermute | solution.py:89
  223.4 3.5 shard_map.246
  234.1 2.9 collective-permute-done.27.side
  244.5 3.7 shard_map.247
  248.2 10.8 %shard_map.248 = (bf16[192,960]{1,0:T(8,128)(2,1)S(1)}, bf16[192,960]{1,0:T(8,128)(2,1)S(1)}, bf16[192,960]{1,0:T(8,128)(2,1)S(1)}, bf16[2,96,2560]{2,1,0:T(8,12...) custom-call(bf16[2560,960]{1,0:T(8,128)(2,1)S(1)} %bitcast.70, bf16[2560,960]{1,0:T(8,128)(2,1)S(1)} %bitcast.74, ...), custom_call_target="tpu_custom_call" | custom-call | flops 383333344 | bytes 1230000 | tf_op jit(solution)/shard_map/pallas_call | solution.py:521
  260.0 3.3 collective-permute-done.34.own_ref.refs_6_
  265.3 9.9 %shard_map.249 = (bf16[192,960]{1,0:T(8,128)(2,1)S(1)}, bf16[192,960]{1,0:T(8,128)(2,1)S(1)}, bf16[192,960]{1,0:T(8,128)(2,1)S(1)}, bf16[2,96,2560]{2,1,0:T(8,12...) custom-call(bf16[2560,960]{1,0:T(8,128)(2,1)S(1)} %bitcast.71, bf16[2560,960]{1,0:T(8,128)(2,1)S(1)} %bitcast.75, ...), custom_call_target="tpu_custom_call" | custom-call | flops 383333344 | bytes 1230000 | tf_op jit(solution)/shard_map/pallas_call | solution.py:521
  275.2 9.9 %shard_map.250 = (bf16[192,960]{1,0:T(8,128)(2,1)S(1)}, bf16[192,960]{1,0:T(8,128)(2,1)S(1)}, bf16[192,960]{1,0:T(8,128)(2,1)S(1)}, bf16[2,96,2560]{2,1,0:T(8,12...) custom-call(bf16[2560,960]{1,0:T(8,128)(2,1)S(1)} %bitcast.72, bf16[2560,960]{1,0:T(8,128)(2,1)S(1)} %bitcast.76, ...), custom_call_target="tpu_custom_call" | custom-call | flops 383333344 | bytes 1230000 | tf_op jit(solution)/shard_map/pallas_call | solution.py:521
  287.4 10.0 %shard_map.251 = (bf16[192,960]{1,0:T(8,128)(2,1)S(1)}, bf16[192,960]{1,0:T(8,128)(2,1)S(1)}, bf16[192,960]{1,0:T(8,128)(2,1)S(1)}, bf16[2,96,2560]{2,1,0:T(8,12...) custom-call(bf16[2560,960]{1,0:T(8,128)(2,1)S(1)} %bitcast.73, bf16[2560,960]{1,0:T(8,128)(2,1)S(1)} %bitcast.77, ...), custom_call_target="tpu_custom_call" | custom-call | flops 383333344 | bytes 1230000 | tf_op jit(solution)/shard_map/pallas_call | solution.py:521
  297.4 7.5 %shard_map.252 = (bf16[4,2,160,960]{3,2,1,0:T(8,128)(2,1)S(1)}, bf16[1,160,960]{2,1,0:T(8,128)(2,1)S(1)}, bf16[1,160,960]{2,1,0:T(8,128)(2,1)S(1)}, bf16[1,160,9...) custom-call(s32[4]{0:T(128)S(1)} %pad_add_fusion.ranks_ref, ...), custom_call_target="tpu_custom_call" | custom-call | flops 191666672 | bytes 615000 | tf_op jit(solution)/shard_map/pallas_call | solution.py:116
  304.9 4.4 collective-permute-done.40.refs_1_
  317.1 14.0 %shard_map.255 = (bf16[4,2,160,960]{3,2,1,0:T(8,128)(2,1)S(1)}, bf16[4,2,160,960]{3,2,1,0:T(8,128)(2,1)S(1)}, bf16[2,160,960]{2,1,0:T(8,128)(2,1)S(1)}, bf16[2,1...) custom-call(s32[4]{0:T(128)S(1)} %pad_add_fusion.ranks_ref, ...), custom_call_target="tpu_custom_call" | custom-call | flops 383333344 | bytes 1230000 | tf_op jit(solution)/shard_map/pallas_call | solution.py:116
  342.5 17.0 %collective-permute-done.56.refs_2_ = bf16[2,96,2560]{2,1,0:T(8,128)(2,1)S(1)} collective-permute-done((bf16[2,96,2560]{2,1,0:T(8,128)(2,1)S(1)}, bf16[2,96,2560]{2,1,0:T(8,128)(2,1)S(1)}, u32[]{:S(2)}, u32[]{:S(2)}) %collective-permute-start.56) | collective-permute-done | bytes 983072 | tf_op jit(solution)/shard_map/ppermute | solution.py:89
  362.8 3.7 collective-permute-done.59.refs_0_
  370.7 4.9 all-to-all-start.3
  379.6 3.1 shard_map.261
  383.7 4.6 collective-permute-done.58.held_ref
  388.3 3.0 shard_map.259
  399.1 5.2 collective-permute-done.65
  412.8 5.7 shard_map.265
  421.2 3.4 collective-permute-done.68.refs_1_
  426.5 4.8 all-to-all-start.4
  437.6 4.8 shard_map.267
  449.2 3.4 shard_map.268
  454.3 4.8 all-to-all-done.4.parts_ref
  459.2 3.2 copy-done.3
  462.4 4.7 shard_map.269
  469.1 8.8 %collective-permute-done.73.refs_0_ = bf16[2,160,1536]{2,1,0:T(8,128)(2,1)S(1)} collective-permute-done((bf16[2,160,1536]{2,1,0:T(8,128)(2,1)}, bf16[2,160,1536]{2,1,0:T(8,128)(2,1)S(1)}, u32[]{:S(2)}, u32[]{:S(2)}) %collective-permute-start.73) | collective-permute-done | bytes 983072 | tf_op jit(solution)/shard_map/ppermute | solution.py:80
  481.6 5.4 all-to-all-start.5
  490.2 4.6 shard_map.270
  516.9 2.8 collective-permute-start.87
  519.7 6.5 %collective-permute-done.83.refs_0_ = bf16[160,1536]{1,0:T(8,128)(2,1)} collective-permute-done((bf16[160,1536]{1,0:T(8,128)(2,1)}, bf16[160,1536]{1,0:T(8,128)(2,1)}, u32[]{:S(2)}, u32[]{:S(2)}) %collective-permute-start.83) | collective-permute-done | bytes 491552 | tf_op jit(solution)/shard_map/ppermute | solution.py:89
  528.1 4.5 collective-permute-start.91
  532.6 4.9 copy.50
  538.3 4.7 collective-permute-done.86
  557.2 12.6 %collective-permute-done.90.refs_0_ = bf16[160,1280]{1,0:T(8,128)(2,1)S(1)} collective-permute-done((bf16[160,1280]{1,0:T(8,128)(2,1)S(1)}, bf16[160,1280]{1,0:T(8,128)(2,1)S(1)}, u32[]{:S(2)}, u32[]{:S(2)}) %collective-permute-start.90) | collective-permute-done | bytes 409632 | tf_op jit(solution)/shard_map/ppermute | solution.py:89
  571.9 3.0 shard_map.284
  576.0 4.4 collective-permute-done.92.refs_0_
  583.5 6.8 %collective-permute-done.93.refs_0_ = bf16[160,1280]{1,0:T(8,128)(2,1)S(1)} collective-permute-done((bf16[160,1280]{1,0:T(8,128)(2,1)S(1)}, bf16[160,1280]{1,0:T(8,128)(2,1)S(1)}, u32[]{:S(2)}, u32[]{:S(2)}) %collective-permute-start.93) | collective-permute-done | bytes 409632 | tf_op jit(solution)/shard_map/ppermute | solution.py:89
  (466 shorter events, 194.5 us)
Async XLA Ops:
  2.8 25.2 %collective-permute-start = (bf16[160,2816]{1,0:T(8,128)(2,1)S(1)}, bf16[160,2816]{1,0:T(8,128)(2,1)}, u32[]{:S(2)}, u32[]{:S(2)}) collective-permute-start(bf16[160,2816]{1,0:T(8,128)(2,1)S(1)} %pad_maximum_fusion.refs_0_), channel_id=1, source_target_pairs={{0,8},{2,10},{4,12},{6,14},{8,16},{10,18},{12,20},{14,22},{16,24},... | collective-permute-start | bytes 2703368 | tf_op jit(solution)/shard_map/ppermute | solution.py:89
  5.8 22.1 %collective-permute-start.1 = (bf16[160,2816]{1,0:T(8,128)(2,1)S(1)}, bf16[160,2816]{1,0:T(8,128)(2,1)}, u32[]{:S(2)}, u32[]{:S(2)}) collective-permute-start(bf16[160,2816]{1,0:T(8,128)(2,1)S(1)} %pad_maximum_fusion.refs_0_), channel_id=1, source_target_pairs={{0,4},{2,6},{4,0},{6,2},{8,12},{10,14},{12,8},{14,10},{16,20},{18,... | collective-permute-start | bytes 2703368 | tf_op jit(solution)/shard_map/ppermute | solution.py:80
  7.4 24.2 %collective-permute-start.2 = (bf16[160,2816]{1,0:T(8,128)(2,1)S(1)}, bf16[160,2816]{1,0:T(8,128)(2,1)S(1)}, u32[]{:S(2)}, u32[]{:S(2)}) collective-permute-start(bf16[160,2816]{1,0:T(8,128)(2,1)S(1)} %pad_maximum_fusion.refs_0_), channel_id=1, source_target_pairs={{0,2},{2,0},{4,6},{6,4},{8,10},{10,8},{12,14},{14,12},{16,18},{18,... | collective-permute-start | bytes 2703368 | tf_op jit(solution)/shard_map/ppermute | solution.py:83
  28.0 26.1 %collective-permute-start.4 = (bf16[160,2816]{1,0:T(8,128)(2,1)}, bf16[160,2816]{1,0:T(8,128)(2,1)}, u32[]{:S(2)}, u32[]{:S(2)}) collective-permute-start(bf16[160,2816]{1,0:T(8,128)(2,1)} %collective-permute-done.refs_0_), channel_id=1, source_target_pairs={{0,2},{2,0},{4,6},{6,4},{8,10},{10,8},{12,14},{14,12},{16,18},{18,... | collective-permute-start | bytes 2703368 | tf_op jit(solution)/shard_map/ppermute | solution.py:83
  28.0 26.1 %collective-permute-start.6 = (bf16[160,2816]{1,0:T(8,128)(2,1)}, bf16[160,2816]{1,0:T(8,128)(2,1)}, u32[]{:S(2)}, u32[]{:S(2)}) collective-permute-start(bf16[160,2816]{1,0:T(8,128)(2,1)} %collective-permute-done.refs_0_), channel_id=1, source_target_pairs={{0,8},{2,10},{4,12},{6,14},{8,16},{10,18},{12,20},{14,22},{16,24},... | collective-permute-start | bytes 2703368 | tf_op jit(solution)/shard_map/ppermute | solution.py:89
  29.0 25.1 %collective-permute-start.7 = (bf16[160,2816]{1,0:T(8,128)(2,1)}, bf16[160,2816]{1,0:T(8,128)(2,1)}, u32[]{:S(2)}, u32[]{:S(2)}) collective-permute-start(bf16[160,2816]{1,0:T(8,128)(2,1)} %collective-permute-done.refs_0_), channel_id=1, source_target_pairs={{0,4},{2,6},{4,0},{6,2},{8,12},{10,14},{12,8},{14,10},{16,20},{18,... | collective-permute-start | bytes 2703368 | tf_op jit(solution)/shard_map/ppermute | solution.py:80
  30.5 18.2 %collective-permute-start.3 = (bf16[160,2816]{1,0:T(8,128)(2,1)}, bf16[160,2816]{1,0:T(8,128)(2,1)}, u32[]{:S(2)}, u32[]{:S(2)}) collective-permute-start(bf16[160,2816]{1,0:T(8,128)(2,1)} %collective-permute-done.1.refs_1_), channel_id=1, source_target_pairs={{0,2},{2,0},{4,6},{6,4},{8,10},{10,8},{12,14},{14,12},{16,18},{18,... | collective-permute-start | bytes 2703368 | tf_op jit(solution)/shard_map/ppermute | solution.py:83
  31.5 22.5 %collective-permute-start.5 = (bf16[96,2560]{1,0:T(8,128)(2,1)S(1)}, bf16[96,2560]{1,0:T(8,128)(2,1)}, u32[]{:S(2)}, u32[]{:S(2)}) collective-permute-start(bf16[96,2560]{1,0:T(8,128)(2,1)S(1)} %bitcast.84), channel_id=1, source_target_pairs={{0,1},{1,0},{2,3},{3,2},{4,5},{5,4},{6,7},{7,6},{8,9},{9,8},{10,11... | collective-permute-start | bytes 1474568 | tf_op jit(solution)/shard_map/ppermute | solution.py:86
  54.4 24.3 %collective-permute-start.10 = (bf16[160,2816]{1,0:T(8,128)(2,1)}, bf16[160,2816]{1,0:T(8,128)(2,1)}, u32[]{:S(2)}, u32[]{:S(2)}) collective-permute-start(bf16[160,2816]{1,0:T(8,128)(2,1)} %collective-permute-done.6.refs_0_), channel_id=1, source_target_pairs={{0,8},{2,10},{4,12},{6,14},{8,16},{10,18},{12,20},{14,22},{16,24},... | collective-permute-start | bytes 2703368 | tf_op jit(solution)/shard_map/ppermute | solution.py:89
  55.9 22.7 %collective-permute-start.11 = (bf16[160,2816]{1,0:T(8,128)(2,1)}, bf16[160,2816]{1,0:T(8,128)(2,1)}, u32[]{:S(2)}, u32[]{:S(2)}) collective-permute-start(bf16[160,2816]{1,0:T(8,128)(2,1)} %collective-permute-done.6.refs_0_), channel_id=1, source_target_pairs={{0,4},{2,6},{4,0},{6,2},{8,12},{10,14},{12,8},{14,10},{16,20},{18,... | collective-permute-start | bytes 2703368 | tf_op jit(solution)/shard_map/ppermute | solution.py:80
  78.7 34.8 %all-to-all-start = ((bf16[4,160,960]{2,1,0:T(8,128)(2,1)}), bf16[4,160,960]{2,1,0:T(8,128)(2,1)S(1)}, u32[]{:S(2)}, u32[]{:S(2)}) async-start(bf16[4,160,960]{2,1,0:T(8,128)(2,1)} %bitcast.103), calls=%async_computation | async-start | bytes 2621440 | tf_op jit(solution)/shard_map/all_to_all | solution.py:93
  82.8 22.3 %collective-permute-start.14 = (bf16[160,2816]{1,0:T(8,128)(2,1)}, bf16[160,2816]{1,0:T(8,128)(2,1)}, u32[]{:S(2)}, u32[]{:S(2)}) collective-permute-start(bf16[160,2816]{1,0:T(8,128)(2,1)} %collective-permute-done.10.refs_0_), channel_id=1, source_target_pairs={{0,4},{2,6},{4,0},{6,2},{8,12},{10,14},{12,8},{14,10},{16,20},{18,... | collective-permute-start | bytes 2703368 | tf_op jit(solution)/shard_map/ppermute | solution.py:80
  113.5 35.2 %all-to-all-start.1 = ((bf16[4,160,960]{2,1,0:T(8,128)(2,1)}), bf16[4,160,960]{2,1,0:T(8,128)(2,1)}, u32[]{:S(2)}, u32[]{:S(2)}) async-start(bf16[4,160,960]{2,1,0:T(8,128)(2,1)} %bitcast.105), calls=%async_computation.1 | async-start | bytes 2621440 | tf_op jit(solution)/shard_map/all_to_all | solution.py:93
  129.0 29.9 %collective-permute-start.15 = (bf16[4,160,960]{2,1,0:T(8,128)(2,1)S(1)}, bf16[4,160,960]{2,1,0:T(8,128)(2,1)}, u32[]{:S(2)}, u32[]{:S(2)}) collective-permute-start(bf16[4,160,960]{2,1,0:T(8,128)(2,1)S(1)} %all-to-all-done.own), channel_id=1, source_target_pairs={{0,4},{2,6},{4,0},{6,2},{8,12},{10,14},{12,8},{14,10},{16,20},{18,... | collective-permute-start | bytes 3686408 | tf_op jit(solution)/shard_map/ppermute | solution.py:80
  148.7 56.7 %all-to-all-start.2 = ((bf16[4,160,960]{2,1,0:T(8,128)(2,1)}), bf16[4,160,960]{2,1,0:T(8,128)(2,1)}, u32[]{:S(2)}, u32[]{:S(2)}) async-start(bf16[4,160,960]{2,1,0:T(8,128)(2,1)} %bitcast.104), calls=%async_computation.2 | async-start | bytes 2621440 | tf_op jit(solution)/shard_map/all_to_all | solution.py:93
  153.4 25.8 %collective-permute-start.16 = (bf16[4,160,960]{2,1,0:T(8,128)(2,1)S(1)}, bf16[4,160,960]{2,1,0:T(8,128)(2,1)S(1)}, u32[]{:S(2)}, u32[]{:S(2)}) collective-permute-start(bf16[4,160,960]{2,1,0:T(8,128)(2,1)S(1)} %all-to-all-done.own), channel_id=1, source_target_pairs={{0,2},{2,0},{4,6},{6,4},{8,10},{10,8},{12,14},{14,12},{16,18},{18,... | collective-permute-start | bytes 3686408 | tf_op jit(solution)/shard_map/ppermute | solution.py:83
  158.9 21.7 %collective-permute-start.19 = (bf16[4,160,960]{2,1,0:T(8,128)(2,1)}, bf16[4,160,960]{2,1,0:T(8,128)(2,1)S(1)}, u32[]{:S(2)}, u32[]{:S(2)}) collective-permute-start(bf16[4,160,960]{2,1,0:T(8,128)(2,1)} %collective-permute-done.15.side), channel_id=1, source_target_pairs={{0,2},{2,0},{4,6},{6,4},{8,10},{10,8},{12,14},{14,12},{16,18},{18,... | collective-permute-start | bytes 3686408 | tf_op jit(solution)/shard_map/ppermute | solution.py:83
  158.9 46.5 %collective-permute-start.20 = (bf16[4,160,960]{2,1,0:T(8,128)(2,1)}, bf16[4,160,960]{2,1,0:T(8,128)(2,1)}, u32[]{:S(2)}, u32[]{:S(2)}) collective-permute-start(bf16[4,160,960]{2,1,0:T(8,128)(2,1)} %all-to-all-done.1.own), channel_id=1, source_target_pairs={{0,4},{2,6},{4,0},{6,2},{8,12},{10,14},{12,8},{14,10},{16,20},{18,... | collective-permute-start | bytes 3686408 | tf_op jit(solution)/shard_map/ppermute | solution.py:80
  159.4 13.6 %collective-permute-start.22 = (bf16[96,2560]{1,0:T(8,128)(2,1)}, bf16[96,2560]{1,0:T(8,128)(2,1)S(1)}, u32[]{:S(2)}, u32[]{:S(2)}) collective-permute-start(bf16[96,2560]{1,0:T(8,128)(2,1)} %copy-done.83), channel_id=1, source_target_pairs={{0,1},{1,0},{2,3},{3,2},{4,5},{5,4},{6,7},{7,6},{8,9},{9,8},{10,11... | collective-permute-start | bytes 1474568 | tf_op jit(solution)/shard_map/ppermute | solution.py:86
  176.3 12.8 %collective-permute-start.23 = (bf16[96,2560]{1,0:T(8,128)(2,1)}, bf16[96,2560]{1,0:T(8,128)(2,1)S(1)}, u32[]{:S(2)}, u32[]{:S(2)}) collective-permute-start(bf16[96,2560]{1,0:T(8,128)(2,1)} %get-tuple-element.467.own_ref.refs_0_), channel_id=1, source_target_pairs={{0,1},{1,0},{2,3},{3,2},{4,5},{5,4},{6,7},{7,6},{8,9},{9,8},{10,11... | collective-permute-start | bytes 1474568 | tf_op jit(solution)/shard_map/ppermute | solution.py:86
  177.4 27.9 %collective-permute-start.25 = (bf16[96,2560]{1,0:T(8,128)(2,1)S(1)}, bf16[96,2560]{1,0:T(8,128)(2,1)}, u32[]{:S(2)}, u32[]{:S(2)}) collective-permute-start(bf16[96,2560]{1,0:T(8,128)(2,1)S(1)} %bitcast.85), channel_id=1, source_target_pairs={{0,8},{2,10},{4,12},{6,14},{8,16},{10,18},{12,20},{14,22},{16,24},... | collective-permute-start | bytes 1474568 | tf_op jit(solution)/shard_map/ppermute | solution.py:89
  179.2 26.2 %collective-permute-start.24 = (bf16[96,2560]{1,0:T(8,128)(2,1)}, bf16[96,2560]{1,0:T(8,128)(2,1)}, u32[]{:S(2)}, u32[]{:S(2)}) collective-permute-start(bf16[96,2560]{1,0:T(8,128)(2,1)} %get-tuple-element.467.own_ref.refs_0_), channel_id=1, source_target_pairs={{0,8},{2,10},{4,12},{6,14},{8,16},{10,18},{12,20},{14,22},{16,24},... | collective-permute-start | bytes 1474568 | tf_op jit(solution)/shard_map/ppermute | solution.py:89
  180.6 26.4 %collective-permute-start.21 = (bf16[4,160,960]{2,1,0:T(8,128)(2,1)}, bf16[4,160,960]{2,1,0:T(8,128)(2,1)}, u32[]{:S(2)}, u32[]{:S(2)}) collective-permute-start(bf16[4,160,960]{2,1,0:T(8,128)(2,1)} %all-to-all-done.1.own), channel_id=1, source_target_pairs={{0,2},{2,0},{4,6},{6,4},{8,10},{10,8},{12,14},{14,12},{16,18},{18,... | collective-permute-start | bytes 3686408 | tf_op jit(solution)/shard_map/ppermute | solution.py:83
  205.4 18.0 %collective-permute-start.26 = (bf16[4,160,960]{2,1,0:T(8,128)(2,1)}, bf16[4,160,960]{2,1,0:T(8,128)(2,1)S(1)}, u32[]{:S(2)}, u32[]{:S(2)}) collective-permute-start(bf16[4,160,960]{2,1,0:T(8,128)(2,1)} %collective-permute-done.20.side), channel_id=1, source_target_pairs={{0,2},{2,0},{4,6},{6,4},{8,10},{10,8},{12,14},{14,12},{16,18},{18,... | collective-permute-start | bytes 3686408 | tf_op jit(solution)/shard_map/ppermute | solution.py:83
  205.5 31.5 %collective-permute-start.27 = (bf16[4,160,960]{2,1,0:T(8,128)(2,1)}, bf16[4,160,960]{2,1,0:T(8,128)(2,1)}, u32[]{:S(2)}, u32[]{:S(2)}) collective-permute-start(bf16[4,160,960]{2,1,0:T(8,128)(2,1)} %all-to-all-done.2.own), channel_id=1, source_target_pairs={{0,4},{2,6},{4,0},{6,2},{8,12},{10,14},{12,8},{14,10},{16,20},{18,... | collective-permute-start | bytes 3686408 | tf_op jit(solution)/shard_map/ppermute | solution.py:80
  206.0 16.2 %collective-permute-start.30 = (bf16[96,2560]{1,0:T(8,128)(2,1)}, bf16[96,2560]{1,0:T(8,128)(2,1)}, u32[]{:S(2)}, u32[]{:S(2)}) collective-permute-start(bf16[96,2560]{1,0:T(8,128)(2,1)} %collective-permute-done.25.dyo_ref.refs_2_), channel_id=1, source_target_pairs={{0,8},{2,10},{4,12},{6,14},{8,16},{10,18},{12,20},{14,22},{16,24},... | collective-permute-start | bytes 1474568 | tf_op jit(solution)/shard_map/ppermute | solution.py:89
  206.0 25.8 %collective-permute-start.29 = (bf16[96,2560]{1,0:T(8,128)(2,1)}, bf16[96,2560]{1,0:T(8,128)(2,1)S(1)}, u32[]{:S(2)}, u32[]{:S(2)}) collective-permute-start(bf16[96,2560]{1,0:T(8,128)(2,1)} %collective-permute-done.24.own_ref.refs_2_), channel_id=1, source_target_pairs={{0,8},{2,10},{4,12},{6,14},{8,16},{10,18},{12,20},{14,22},{16,24},... | collective-permute-start | bytes 1474568 | tf_op jit(solution)/shard_map/ppermute | solution.py:89
  207.0 24.9 %collective-permute-start.32 = (bf16[96,2560]{1,0:T(8,128)(2,1)}, bf16[96,2560]{1,0:T(8,128)(2,1)S(1)}, u32[]{:S(2)}, u32[]{:S(2)}) collective-permute-start(bf16[96,2560]{1,0:T(8,128)(2,1)} %collective-permute-done.25.dyo_ref.refs_2_), channel_id=1, source_target_pairs={{0,1},{1,0},{2,3},{3,2},{4,5},{5,4},{6,7},{7,6},{8,9},{9,8},{10,11... | collective-permute-start | bytes 1474568 | tf_op jit(solution)/shard_map/ppermute | solution.py:86
  223.4 15.2 %collective-permute-start.28 = (bf16[4,160,960]{2,1,0:T(8,128)(2,1)}, bf16[4,160,960]{2,1,0:T(8,128)(2,1)S(1)}, u32[]{:S(2)}, u32[]{:S(2)}) collective-permute-start(bf16[4,160,960]{2,1,0:T(8,128)(2,1)} %all-to-all-done.2.own), channel_id=1, source_target_pairs={{0,2},{2,0},{4,6},{6,4},{8,10},{10,8},{12,14},{14,12},{16,18},{18,... | collective-permute-start | bytes 3686408 | tf_op jit(solution)/shard_map/ppermute | solution.py:83
  237.0 23.0 %collective-permute-start.35 = (bf16[96,2560]{1,0:T(8,128)(2,1)}, bf16[96,2560]{1,0:T(8,128)(2,1)}, u32[]{:S(2)}, u32[]{:S(2)}) collective-permute-start(bf16[96,2560]{1,0:T(8,128)(2,1)} %collective-permute-done.30.dyo_ref.refs_4_), channel_id=1, source_target_pairs={{0,8},{2,10},{4,12},{6,14},{8,16},{10,18},{12,20},{14,22},{16,24},... | collective-permute-start | bytes 1474568 | tf_op jit(solution)/shard_map/ppermute | solution.py:89
  237.0 26.3 %collective-permute-start.34 = (bf16[96,2560]{1,0:T(8,128)(2,1)S(1)}, bf16[96,2560]{1,0:T(8,128)(2,1)}, u32[]{:S(2)}, u32[]{:S(2)}) collective-permute-start(bf16[96,2560]{1,0:T(8,128)(2,1)S(1)} %collective-permute-done.29.own_ref.refs_4_), channel_id=1, source_target_pairs={{0,8},{2,10},{4,12},{6,14},{8,16},{10,18},{12,20},{14,22},{16,24},... | collective-permute-start | bytes 1474568 | tf_op jit(solution)/shard_map/ppermute | solution.py:89
  238.0 25.3 %collective-permute-start.37 = (bf16[96,2560]{1,0:T(8,128)(2,1)}, bf16[96,2560]{1,0:T(8,128)(2,1)}, u32[]{:S(2)}, u32[]{:S(2)}) collective-permute-start(bf16[96,2560]{1,0:T(8,128)(2,1)} %collective-permute-done.30.dyo_ref.refs_4_), channel_id=1, source_target_pairs={{0,1},{1,0},{2,3},{3,2},{4,5},{5,4},{6,7},{7,6},{8,9},{9,8},{10,11... | collective-permute-start | bytes 1474568 | tf_op jit(solution)/shard_map/ppermute | solution.py:86
  239.6 23.7 %collective-permute-start.36 = (bf16[96,2560]{1,0:T(8,128)(2,1)S(1)}, bf16[96,2560]{1,0:T(8,128)(2,1)}, u32[]{:S(2)}, u32[]{:S(2)}) collective-permute-start(bf16[96,2560]{1,0:T(8,128)(2,1)S(1)} %collective-permute-done.29.own_ref.refs_4_), channel_id=1, source_target_pairs={{0,1},{1,0},{2,3},{3,2},{4,5},{5,4},{6,7},{7,6},{8,9},{9,8},{10,11... | collective-permute-start | bytes 1474568 | tf_op jit(solution)/shard_map/ppermute | solution.py:86
  263.3 21.9 %collective-permute-start.39 = (bf16[96,2560]{1,0:T(8,128)(2,1)}, bf16[96,2560]{1,0:T(8,128)(2,1)S(1)}, u32[]{:S(2)}, u32[]{:S(2)}) collective-permute-start(bf16[96,2560]{1,0:T(8,128)(2,1)} %collective-permute-done.35.dyo_ref.refs_6_), channel_id=1, source_target_pairs={{0,1},{1,0},{2,3},{3,2},{4,5},{5,4},{6,7},{7,6},{8,9},{9,8},{10,11... | collective-permute-start | bytes 1474568 | tf_op jit(solution)/shard_map/ppermute | solution.py:86
  263.8 23.1 %collective-permute-start.38 = (bf16[96,2560]{1,0:T(8,128)(2,1)}, bf16[96,2560]{1,0:T(8,128)(2,1)S(1)}, u32[]{:S(2)}, u32[]{:S(2)}) collective-permute-start(bf16[96,2560]{1,0:T(8,128)(2,1)} %collective-permute-done.34.own_ref.refs_6_), channel_id=1, source_target_pairs={{0,1},{1,0},{2,3},{3,2},{4,5},{5,4},{6,7},{7,6},{8,9},{9,8},{10,11... | collective-permute-start | bytes 1474568 | tf_op jit(solution)/shard_map/ppermute | solution.py:86
  286.9 22.5 %collective-permute-start.40 = (bf16[2,96,2560]{2,1,0:T(8,128)(2,1)S(1)}, bf16[2,96,2560]{2,1,0:T(8,128)(2,1)S(1)}, u32[]{:S(2)}, u32[]{:S(2)}) collective-permute-start(bf16[2,96,2560]{2,1,0:T(8,128)(2,1)S(1)} %get-tuple-element.444), channel_id=1, source_target_pairs={{0,1},{1,0},{2,3},{3,2},{4,5},{5,4},{6,7},{7,6},{8,9},{9,8},{10,11... | collective-permute-start | bytes 2949128 | tf_op jit(solution)/shard_map/ppermute | solution.py:86
  309.6 23.4 %collective-permute-start.50 = (bf16[2,96,2560]{2,1,0:T(8,128)(2,1)S(1)}, bf16[2,96,2560]{2,1,0:T(8,128)(2,1)S(1)}, u32[]{:S(2)}, u32[]{:S(2)}) collective-permute-start(bf16[2,96,2560]{2,1,0:T(8,128)(2,1)S(1)} %shard_map.253), channel_id=1, source_target_pairs={{0,8},{2,10},{4,12},{6,14},{8,16},{10,18},{12,20},{14,22},{16,24},... | collective-permute-start | bytes 2949128 | tf_op jit(solution)/shard_map/ppermute | solution.py:89
  309.7 23.4 %collective-permute-start.49 = (bf16[2,96,2560]{2,1,0:T(8,128)(2,1)S(1)}, bf16[2,96,2560]{2,1,0:T(8,128)(2,1)S(1)}, u32[]{:S(2)}, u32[]{:S(2)}) collective-permute-start(bf16[2,96,2560]{2,1,0:T(8,128)(2,1)S(1)} %get-tuple-element.476), channel_id=1, source_target_pairs={{0,1},{1,0},{2,3},{3,2},{4,5},{5,4},{6,7},{7,6},{8,9},{9,8},{10,11... | collective-permute-start | bytes 2949128 | tf_op jit(solution)/shard_map/ppermute | solution.py:86
  334.0 25.5 %collective-permute-start.56 = (bf16[2,96,2560]{2,1,0:T(8,128)(2,1)S(1)}, bf16[2,96,2560]{2,1,0:T(8,128)(2,1)S(1)}, u32[]{:S(2)}, u32[]{:S(2)}) collective-permute-start(bf16[2,96,2560]{2,1,0:T(8,128)(2,1)S(1)} %shard_map.256), channel_id=1, source_target_pairs={{0,8},{2,10},{4,12},{6,14},{8,16},{10,18},{12,20},{14,22},{16,24},... | collective-permute-start | bytes 2949128 | tf_op jit(solution)/shard_map/ppermute | solution.py:89
  334.8 24.7 %collective-permute-start.55 = (bf16[2,96,2560]{2,1,0:T(8,128)(2,1)S(1)}, bf16[2,96,2560]{2,1,0:T(8,128)(2,1)S(1)}, u32[]{:S(2)}, u32[]{:S(2)}) collective-permute-start(bf16[2,96,2560]{2,1,0:T(8,128)(2,1)S(1)} %get-tuple-element.492), channel_id=1, source_target_pairs={{0,1},{1,0},{2,3},{3,2},{4,5},{5,4},{6,7},{7,6},{8,9},{9,8},{10,11... | collective-permute-start | bytes 2949128 | tf_op jit(solution)/shard_map/ppermute | solution.py:86
  336.3 30.3 %collective-permute-start.59 = (bf16[4,160,960]{2,1,0:T(8,128)(2,1)S(1)}, bf16[4,160,960]{2,1,0:T(8,128)(2,1)S(1)}, u32[]{:S(2)}, u32[]{:S(2)}) collective-permute-start(bf16[4,160,960]{2,1,0:T(8,128)(2,1)S(1)} %get-tuple-element.501), channel_id=1, source_target_pairs={{0,4},{2,6},{4,0},{6,2},{8,12},{10,14},{12,8},{14,10},{16,20},{18,... | collective-permute-start | bytes 3686408 | tf_op jit(solution)/shard_map/ppermute | solution.py:80
  361.4 26.9 %collective-permute-start.58 = (bf16[2,96,2560]{2,1,0:T(8,128)(2,1)}, bf16[2,96,2560]{2,1,0:T(8,128)(2,1)}, u32[]{:S(2)}, u32[]{:S(2)}) collective-permute-start(bf16[2,96,2560]{2,1,0:T(8,128)(2,1)} %shard_map.258), channel_id=1, source_target_pairs={{0,8},{2,10},{4,12},{6,14},{8,16},{10,18},{12,20},{14,22},{16,24},... | collective-permute-start | bytes 2949128 | tf_op jit(solution)/shard_map/ppermute | solution.py:89
  361.4 26.9 %collective-permute-start.57 = (bf16[2,96,2560]{2,1,0:T(8,128)(2,1)}, bf16[2,96,2560]{2,1,0:T(8,128)(2,1)}, u32[]{:S(2)}, u32[]{:S(2)}) collective-permute-start(bf16[2,96,2560]{2,1,0:T(8,128)(2,1)} %get-tuple-element.496), channel_id=1, source_target_pairs={{0,1},{1,0},{2,3},{3,2},{4,5},{5,4},{6,7},{7,6},{8,9},{9,8},{10,11... | collective-permute-start | bytes 2949128 | tf_op jit(solution)/shard_map/ppermute | solution.py:86
  366.5 29.7 %collective-permute-start.64 = (bf16[4,160,960]{2,1,0:T(8,128)(2,1)}, bf16[4,160,960]{2,1,0:T(8,128)(2,1)}, u32[]{:S(2)}, u32[]{:S(2)}) collective-permute-start(bf16[4,160,960]{2,1,0:T(8,128)(2,1)} %get-tuple-element.523), channel_id=1, source_target_pairs={{0,4},{2,6},{4,0},{6,2},{8,12},{10,14},{12,8},{14,10},{16,20},{18,... | collective-permute-start | bytes 3686408 | tf_op jit(solution)/shard_map/ppermute | solution.py:80
  370.7 54.8 %all-to-all-start.3 = ((bf16[4,160,960]{2,1,0:T(8,128)(2,1)}), bf16[4,160,960]{2,1,0:T(8,128)(2,1)S(1)}, u32[]{:S(2)}, u32[]{:S(2)}) async-start(bf16[4,160,960]{2,1,0:T(8,128)(2,1)} %copy-done.12), calls=%async_computation.3 | async-start | bytes 2621440 | tf_op jit(solution)/shard_map/all_to_all | solution.py:93
  396.2 14.9 %collective-permute-start.66 = (bf16[2,160,960]{2,1,0:T(8,128)(2,1)S(1)}, bf16[2,160,960]{2,1,0:T(8,128)(2,1)S(1)}, u32[]{:S(2)}, u32[]{:S(2)}) collective-permute-start(bf16[2,160,960]{2,1,0:T(8,128)(2,1)S(1)} %get-tuple-element.533), channel_id=1, source_target_pairs={{0,4},{2,6},{4,0},{6,2},{8,12},{10,14},{12,8},{14,10},{16,20},{18,... | collective-permute-start | bytes 1843208 | tf_op jit(solution)/shard_map/ppermute | solution.py:80
  411.1 13.5 %collective-permute-start.68 = (bf16[2,160,960]{2,1,0:T(8,128)(2,1)S(1)}, bf16[2,160,960]{2,1,0:T(8,128)(2,1)S(1)}, u32[]{:S(2)}, u32[]{:S(2)}) collective-permute-start(bf16[2,160,960]{2,1,0:T(8,128)(2,1)S(1)} %get-tuple-element.540), channel_id=1, source_target_pairs={{0,4},{2,6},{4,0},{6,2},{8,12},{10,14},{12,8},{14,10},{16,20},{18,... | collective-permute-start | bytes 1843208 | tf_op jit(solution)/shard_map/ppermute | solution.py:80
  426.5 32.6 %all-to-all-start.4 = ((bf16[4,160,960]{2,1,0:T(8,128)(2,1)}), bf16[4,160,960]{2,1,0:T(8,128)(2,1)S(1)}, u32[]{:S(2)}, u32[]{:S(2)}) async-start(bf16[4,160,960]{2,1,0:T(8,128)(2,1)} %copy-done.11), calls=%async_computation.4 | async-start | bytes 2621440 | tf_op jit(solution)/shard_map/all_to_all | solution.py:93
  453.9 24.0 %collective-permute-start.73 = (bf16[2,160,1536]{2,1,0:T(8,128)(2,1)}, bf16[2,160,1536]{2,1,0:T(8,128)(2,1)S(1)}, u32[]{:S(2)}, u32[]{:S(2)}) collective-permute-start(bf16[2,160,1536]{2,1,0:T(8,128)(2,1)} %get-tuple-element.568), channel_id=1, source_target_pairs={{0,4},{2,6},{4,0},{6,2},{8,12},{10,14},{12,8},{14,10},{16,20},{18,... | collective-permute-start | bytes 2949128 | tf_op jit(solution)/shard_map/ppermute | solution.py:80
  468.1 19.0 %collective-permute-start.76 = (bf16[2,160,1280]{2,1,0:T(8,128)(2,1)}, bf16[2,160,1280]{2,1,0:T(8,128)(2,1)}, u32[]{:S(2)}, u32[]{:S(2)}) collective-permute-start(bf16[2,160,1280]{2,1,0:T(8,128)(2,1)} %get-tuple-element.575), channel_id=1, source_target_pairs={{0,2},{2,0},{4,6},{6,4},{8,10},{10,8},{12,14},{14,12},{16,18},{18,... | collective-permute-start | bytes 2457608 | tf_op jit(solution)/shard_map/ppermute | solution.py:83
  468.6 18.5 %collective-permute-start.75 = (bf16[2,160,1280]{2,1,0:T(8,128)(2,1)}, bf16[2,160,1280]{2,1,0:T(8,128)(2,1)}, u32[]{:S(2)}, u32[]{:S(2)}) collective-permute-start(bf16[2,160,1280]{2,1,0:T(8,128)(2,1)} %get-tuple-element.573), channel_id=1, source_target_pairs={{0,2},{2,0},{4,6},{6,4},{8,10},{10,8},{12,14},{14,12},{16,18},{18,... | collective-permute-start | bytes 2457608 | tf_op jit(solution)/shard_map/ppermute | solution.py:83
  468.6 18.5 %collective-permute-start.74 = (bf16[2,160,1280]{2,1,0:T(8,128)(2,1)}, bf16[2,160,1280]{2,1,0:T(8,128)(2,1)}, u32[]{:S(2)}, u32[]{:S(2)}) collective-permute-start(bf16[2,160,1280]{2,1,0:T(8,128)(2,1)} %get-tuple-element.571), channel_id=1, source_target_pairs={{0,2},{2,0},{4,6},{6,4},{8,10},{10,8},{12,14},{14,12},{16,18},{18,... | collective-permute-start | bytes 2457608 | tf_op jit(solution)/shard_map/ppermute | solution.py:83
  478.8 23.8 %collective-permute-start.80 = (bf16[2,160,1536]{2,1,0:T(8,128)(2,1)}, bf16[2,160,1536]{2,1,0:T(8,128)(2,1)S(1)}, u32[]{:S(2)}, u32[]{:S(2)}) collective-permute-start(bf16[2,160,1536]{2,1,0:T(8,128)(2,1)} %get-tuple-element.595), channel_id=1, source_target_pairs={{0,4},{2,6},{4,0},{6,2},{8,12},{10,14},{12,8},{14,10},{16,20},{18,... | collective-permute-start | bytes 2949128 | tf_op jit(solution)/shard_map/ppermute | solution.py:80
  480.1 15.9 %collective-permute-start.78 = (bf16[96,2560]{1,0:T(8,128)(2,1)}, bf16[96,2560]{1,0:T(8,128)(2,1)}, u32[]{:S(2)}, u32[]{:S(2)}) collective-permute-start(bf16[96,2560]{1,0:T(8,128)(2,1)} %get-tuple-element.583), channel_id=1, source_target_pairs={{0,1},{1,0},{2,3},{3,2},{4,5},{5,4},{6,7},{7,6},{8,9},{9,8},{10,11... | collective-permute-start | bytes 1474568 | tf_op jit(solution)/shard_map/ppermute | solution.py:86
  481.6 62.9 %all-to-all-start.5 = ((bf16[4,160,960]{2,1,0:T(8,128)(2,1)}), bf16[4,160,960]{2,1,0:T(8,128)(2,1)}, u32[]{:S(2)}, u32[]{:S(2)}) async-start(bf16[4,160,960]{2,1,0:T(8,128)(2,1)} %shard_map.266), calls=%async_computation.5 | async-start | bytes 2621440 | tf_op jit(solution)/shard_map/all_to_all | solution.py:93
  503.6 44.0 %collective-permute-start.84 = (bf16[4,160,1280]{2,1,0:T(8,128)(2,1)}, bf16[4,160,1280]{2,1,0:T(8,128)(2,1)}, u32[]{:S(2)}, u32[]{:S(2)}) collective-permute-start(bf16[4,160,1280]{2,1,0:T(8,128)(2,1)} %get-tuple-element.612), channel_id=1, source_target_pairs={{0,4},{2,6},{4,0},{6,2},{8,12},{10,14},{12,8},{14,10},{16,20},{18,... | collective-permute-start | bytes 4915208 | tf_op jit(solution)/shard_map/ppermute | solution.py:80
  510.9 15.4 %collective-permute-start.83 = (bf16[160,1536]{1,0:T(8,128)(2,1)}, bf16[160,1536]{1,0:T(8,128)(2,1)}, u32[]{:S(2)}, u32[]{:S(2)}) collective-permute-start(bf16[160,1536]{1,0:T(8,128)(2,1)} %shard_map.274), channel_id=1, source_target_pairs={{0,8},{2,10},{4,12},{6,14},{8,16},{10,18},{12,20},{14,22},{16,24},... | collective-permute-start | bytes 1474568 | tf_op jit(solution)/shard_map/ppermute | solution.py:89
  514.5 23.1 %collective-permute-start.85 = (f32[15360]{0:T(1024)S(1)}, f32[15360]{0:T(1024)S(1)}, u32[]{:S(2)}, u32[]{:S(2)}) collective-permute-start(f32[15360]{0:T(1024)S(1)} %add.156), channel_id=1, source_target_pairs={{0,8},{2,10},{4,12},{6,14},{8,16},{10,18},{12,20},{14,22},{16,24},... | collective-permute-start | bytes 184328 | tf_op jit(solution)/shard_map/ppermute | solution.py:89
  515.8 27.2 %collective-permute-start.86 = (f32[15360]{0:T(1024)S(1)}, f32[15360]{0:T(1024)S(1)}, u32[]{:S(2)}, u32[]{:S(2)}) collective-permute-start(f32[15360]{0:T(1024)S(1)} %add.156), channel_id=1, source_target_pairs={{0,16},{2,18},{4,20},{6,22},{8,24},{10,26},{12,28},{14,30},{16,0},... | collective-permute-start | bytes 184328 | tf_op jit(solution)/shard_map/ppermute | solution.py:89
  516.9 26.7 %collective-permute-start.87 = (f32[15360]{0:T(1024)S(1)}, f32[15360]{0:T(1024)}, u32[]{:S(2)}, u32[]{:S(2)}) collective-permute-start(f32[15360]{0:T(1024)S(1)} %add.156), channel_id=1, source_target_pairs={{0,24},{2,26},{4,28},{6,30},{8,0},{10,2},{12,4},{14,6},{16,8},{18,... | collective-permute-start | bytes 184328 | tf_op jit(solution)/shard_map/ppermute | solution.py:89
  528.1 18.1 %collective-permute-start.91 = (bf16[160,1536]{1,0:T(8,128)(2,1)}, bf16[160,1536]{1,0:T(8,128)(2,1)}, u32[]{:S(2)}, u32[]{:S(2)}) collective-permute-start(bf16[160,1536]{1,0:T(8,128)(2,1)} %shard_map.275), channel_id=1, source_target_pairs={{0,8},{2,10},{4,12},{6,14},{8,16},{10,18},{12,20},{14,22},{16,24},... | collective-permute-start | bytes 1474568 | tf_op jit(solution)/shard_map/ppermute | solution.py:89
  550.3 24.6 %collective-permute-start.94 = (bf16[160,1536]{1,0:T(8,128)(2,1)S(1)}, bf16[160,1536]{1,0:T(8,128)(2,1)S(1)}, u32[]{:S(2)}, u32[]{:S(2)}) collective-permute-start(bf16[160,1536]{1,0:T(8,128)(2,1)S(1)} %shard_map.280), channel_id=1, source_target_pairs={{0,8},{2,10},{4,12},{6,14},{8,16},{10,18},{12,20},{14,22},{16,24},... | collective-permute-start | bytes 1474568 | tf_op jit(solution)/shard_map/ppermute | solution.py:89
  554.1 15.6 %collective-permute-start.90 = (bf16[160,1280]{1,0:T(8,128)(2,1)S(1)}, bf16[160,1280]{1,0:T(8,128)(2,1)S(1)}, u32[]{:S(2)}, u32[]{:S(2)}) collective-permute-start(bf16[160,1280]{1,0:T(8,128)(2,1)S(1)} %shard_map.278), channel_id=1, source_target_pairs={{0,8},{2,10},{4,12},{6,14},{8,16},{10,18},{12,20},{14,22},{16,24},... | collective-permute-start | bytes 1228808 | tf_op jit(solution)/shard_map/ppermute | solution.py:89
  554.3 27.2 %collective-permute-start.88 = (bf16[96,2560]{1,0:T(8,128)(2,1)S(1)}, bf16[96,2560]{1,0:T(8,128)(2,1)S(1)}, u32[]{:S(2)}, u32[]{:S(2)}) collective-permute-start(bf16[96,2560]{1,0:T(8,128)(2,1)S(1)} %copy-done.78), channel_id=1, source_target_pairs={{0,1},{1,0},{2,3},{3,2},{4,5},{5,4},{6,7},{7,6},{8,9},{9,8},{10,11... | collective-permute-start | bytes 1474568 | tf_op jit(solution)/shard_map/ppermute | solution.py:86
  (139 other events, 810.0 us)
where the time goes:
time: 602 us; the launch traced here: 591 us
  waiting for transfers between devices  231 us (38%)
  Pallas kernels  159 us (26%)
  starting transfers between devices  95.1 us (16%)
  local copies, waits for them, and re-layouts  93.8 us (16%)
  other arithmetic  11.1 us (2%)
    ppermute x21, waiting for transfers between devices, next_z(): return lax.ppermute(self.gate(value), 'dp', self.ring(step))  104 us
    pallas_call x33, Pallas kernels, call(): pl.pallas_call(body, out_shape=[jax.ShapeDtypeStruct(shape, dtype) for sh...  102 us
    unnamed x205, local copies, waits for them, and re-layouts  65.3 us
    pallas_call x15, Pallas kernels, in_vmem(): pl.pallas_call(body, out_shape=[jax.ShapeDtypeStruct(shape, dtype) for sh...  57.2 us
    ppermute x15, waiting for transfers between devices, over_y(): return lax.ppermute(self.gate(value), 'dp', self.swap_y)  41.8 us
    all_to_all x6, waiting for transfers between devices, along_z(): lax.all_to_all(value, 'dp', 0, 0, axis_index_groups=self.lines, tiled=True)  37 us
    ppermute x21, waiting for transfers between devices, over_x(): return lax.ppermute(self.gate(value), 'mp', [(0, 1), (1, 0)])  32 us
    all_to_all x6, starting transfers between devices, along_z(): lax.all_to_all(value, 'dp', 0, 0, axis_index_groups=self.lines, tiled=True)  27.7 us
  transfers between devices with their start and end apart: 102, of which 49 were waited for; matrix products, arithmetic and copies ran while one was open for 7% of the time, Pallas kernels for 27%

commit v1 on v0

--- a/solution.py
+++ b/solution.py
@@ -778,8 +778,13 @@
     up_back.append(grid.over_y(up_away[1]))
     query_keep, query_send = product_rows(ranks, [grid.gate(normed)], [[grad_query]], count)[0]
     grid.wait(grad_other, query_keep, up_back[1])
+    query_got = [grid.over_c(send) for send in query_send]
     grid.wait(down_parts)
     gate_parts = grid.along_z(gate_rows)
+    grid.wait(*query_got)
+    query_away, query_stay = own_rows(ranks, grid.gate(query_keep), query_got, 2)
+    grid.wait(*query_away)
+    query_back = [grid.over_y(query_away[0])]
     up_rows = plus(grid.gate(up_stay), *up_back)
     grid.wait(up_rows)
     grad_keyval = (grad_own + grad_other).astype(BF16)
@@ -787,24 +792,25 @@
         ranks, [grid.gate(grad_resid_b), normed], [[mixed_b, grad_keyval]], count, beside=True
     )[0]
     grid.wait(out_keep)
+    mine, other = product_nt(
+        ranks, jnp.concatenate([grad_query, grid.gate(grad_keyval)], axis=1), w_qkv, micro
+    )
+    grid.wait(mine)
+    grad_normed = grid.over_x(other)
     out_got = [grid.over_c(send) for send in out_send]
+    grid.wait(gate_parts)
+    up_parts = grid.along_z(up_rows)
+    grid.wait(query_back[0])
+    query_back.append(grid.over_y(query_away[1]))
     grid.wait(*out_got)
     out_away, out_stay = own_rows(ranks, grid.gate(out_keep), out_got, 2)
     grid.wait(*out_away)
+    grid.wait(query_back[1])
     out_back = [grid.over_y(out_away[0])]
-    grid.wait(gate_parts)
-    up_parts = grid.along_z(up_rows)
-    mine, other = product_nt(
-        ranks, jnp.concatenate([grad_query, grid.gate(grad_keyval)], axis=1), w_qkv, micro
-    )
-    grid.wait(mine)
-    grad_normed = grid.over_x(other)
-    query_got = [grid.over_c(send) for send in query_send]
-    grid.wait(out_back[0])
-    out_back.append(grid.over_y(out_away[1]))
-    grid.wait(*query_got)
-    query_away, query_stay = own_rows(ranks, grid.gate(query_keep), query_got)
-    grid.wait(query_away)
+    query_rows = plus(grid.gate(query_stay), *query_back)
+    query_held = ring_sum(grid, query_rows, None, 1)
+    grid.wait(query_held)
+    query_held = grid.next_z(query_held)
     grid.wait(grad_normed)
     grad_input, gain_attn_term = in_vmem(
         first_norm_back,
@@ -819,14 +825,6 @@
     grid.wait(narrow)
     narrow_other = grid.over_x(narrow)
     outputs_other = grid.over_x(outputs)
-    down_grad = collect_columns(grid.gate(down_parts), True)
-    grid.wait(down_grad)
-    grid.wait(out_back[1])
-    query_back = grid.over_y(query_away)
-    out_rows = plus(grid.gate(out_stay), *out_back)
-    out_held = ring_sum(grid, out_rows, None, 1)
-    grid.wait(out_held)
-    out_held = grid.next_z(out_held)
 
     ffn = b_gate.shape[0]
     wide = jnp.zeros((2, ffn), F32)
@@ -834,53 +832,52 @@
     grid.wait(narrow_other)
     small = jnp.concatenate([(narrow + narrow_other).reshape(-1), wide])
     small_other = grid.over_c(small)
-    grid.wait(small_other)
+    down_grad = collect_columns(grid.gate(down_parts), True)
+    grid.wait(down_grad, small_other)
     small = small + small_other
     grid.wait(small)
+    grid.wait(up_parts)
+    grid.wait(query_held)
+    query_held = ring_sum(grid, query_rows, query_held, 2)
+    grid.wait(query_held)
+    query_held = grid.next_z(query_held)
+    grid.wait(out_back[0])
+    out_back.append(grid.over_y(out_away[1]))
     small_all = [small] + [grid.next_z(small, step) for step in range(1, count)]
-    grid.wait(out_held)
-    out_held = ring_sum(grid, out_rows, out_held, 2)
+    gate_grad = collect_columns(grid.gate(gate_parts))
+    grid.wait(gate_grad)
+    for step in range(3, count):
+        grid.wait(query_held)
+        query_held = ring_sum(grid, query_rows, query_held, step)
+        grid.wait(query_held)
+        query_held = grid.next_z(query_held)
+    grid.wait(*out_back)
+    out_rows = plus(grid.gate(out_stay), *out_back)
+    out_held = ring_sum(grid, out_rows, None, 1)
     grid.wait(out_held)
     out_held = grid.next_z(out_held)
-    grid.wait(up_parts)
-    gate_grad = collect_columns(grid.gate(gate_parts))
-    grid.wait(gate_grad)
-    grid.wait(query_back)
-    query_rows = plus(grid.gate(query_stay), query_back)
-    query_held = ring_sum(grid, query_rows, None, 1)
-    grid.wait(query_held)
-    query_held = grid.next_z(query_held)
     grid.wait(outputs_other, *small_all)
     places = [lax.rem(grid.z - z + count, count) for z in range(count)]
     small = sum(pick(small_all, place) for place in places)
     grid.wait(small)
     small_other = grid.over_y(small)
     grad_input_other = grid.over_x(grad_input)
-    for step in range(3, count):
+    for step in range(2, count):
         grid.wait(out_held)
         out_held = ring_sum(grid, out_rows, out_held, step)
         grid.wait(out_held)
         out_held = grid.next_z(out_held)
-    grid.wait(query_held)
-    query_held = ring_sum(grid, query_rows, query_held, 2)
-    grid.wait(query_held)
-    query_held = grid.next_z(query_held)
+    query_grad = ring_sum(grid, query_rows, grid.gate(query_held), count)
+    grid.wait(query_grad)
     up_grad = collect_columns(grid.gate(up_parts))
-    grid.wait(up_grad)
+    grid.wait(up_grad, small_other)
+    small = small + small_other
     grid.wait(out_held)
     out_held = ring_sum(grid, out_rows, out_held, count)
     grid.wait(out_held)
     keyval_grad = out_held[:, query_width:]
     keyval_other = grid.over_x(keyval_grad)
     out_grad = out_held[:, :query_width].T
-    for step in range(3, count):
-        grid.wait(query_held)
-        query_held = ring_sum(grid, query_rows, query_held, step)
-        grid.wait(query_held)
-        query_held = grid.next_z(query_held)
-    grid.wait(out_grad, keyval_other, grad_input_other)
-    small = small + small_other
-    query_grad = ring_sum(grid, query_rows, grid.gate(query_held), count)
     keyval_grad = pair(grid.x, keyval_grad, keyval_other, 1)
     keyval_grad = keyval_grad.reshape(keyval_grad.shape[0], 2 * head_dim)
     return (

time: 602 us -> 598 us (level)
  waiting for transfers between devices: 231 us -> 238 us
    ppermute x21, starting transfers between devices: 27.6 us -> 20.3 us  [next_z(): return lax.ppermute(self.gate(value), 'dp', self.ring(step))]
    unnamed x205 -> x209, local copies, waits for them, and re-layouts: 65.3 us -> 59.5 us
    ppermute x15 -> x16, waiting for transfers between devices: 41.8 us -> 45.3 us  [over_y(): return lax.ppermute(self.gate(value), 'dp', self.swap_y)]
  transfers between devices with their start and end apart: 102 -> 103, of which waited for: 49 -> 53; matrix products, arithmetic and copies ran while one was open for 7% -> 7% of each run, Pallas kernels for 27% -> 27%
where the time goes in v1:
time: 598 us; the launch traced here: 588 us
  waiting for transfers between devices  238 us (40%)
  Pallas kernels  159 us (27%)
  starting transfers between devices  89.6 us (15%)
  local copies, waits for them, and re-layouts  87.9 us (15%)
  other arithmetic  10.6 us (2%)
    ppermute x21, waiting for transfers between devices, next_z(): return lax.ppermute(self.gate(value), 'dp', self.ring(step))  107 us
    pallas_call x33, Pallas kernels, call(): pl.pallas_call(body, out_shape=[jax.ShapeDtypeStruct(shape, dtype) for sh...  101 us
    unnamed x209, local copies, waits for them, and re-layouts  59.5 us
    pallas_call x15, Pallas kernels, in_vmem(): pl.pallas_call(body, out_shape=[jax.ShapeDtypeStruct(shape, dtype) for sh...  58.4 us
    ppermute x16, waiting for transfers between devices, over_y(): return lax.ppermute(self.gate(value), 'dp', self.swap_y)  45.3 us
    all_to_all x6, waiting for transfers between devices, along_z(): lax.all_to_all(value, 'dp', 0, 0, axis_index_groups=self.lines, tiled=True)  37 us
    ppermute x21, waiting for transfers between devices, over_x(): return lax.ppermute(self.gate(value), 'mp', [(0, 1), (1, 0)])  35.7 us
    all_to_all x6, starting transfers between devices, along_z(): lax.all_to_all(value, 'dp', 0, 0, axis_index_groups=self.lines, tiled=True)  27.5 us
  transfers between devices with their start and end apart: 103, of which 53 were waited for; matrix products, arithmetic and copies ran while one was open for 7% of the time, Pallas kernels for 27%

profile of v1, /device:TPU:0, one launch (start us, length us, event | category | flops | bytes accessed | tf_op | source)
XLA Modules:
  0.0 587.7 jit_solution(14744492546137393395)
XLA Ops:
  2.8 3.1 collective-permute-start
  10.0 2.8 copy.61
  15.4 12.5 %collective-permute-done.refs_0_ = bf16[160,2816]{1,0:T(8,128)(2,1)} collective-permute-done((bf16[160,2816]{1,0:T(8,128)(2,1)S(1)}, bf16[160,2816]{1,0:T(8,128)(2,1)}, u32[]{:S(2)}, u32[]{:S(2)}) %collective-permute-start) | collective-permute-done | bytes 901152 | tf_op jit(solution)/shard_map/ppermute | solution.py:89
  33.1 4.4 reshape.230
  40.4 4.4 reshape.233
  50.1 4.0 shard_map.237
  59.1 4.3 shard_map.238
  64.4 14.4 %collective-permute-done.10.refs_0_ = bf16[160,2816]{1,0:T(8,128)(2,1)} collective-permute-done((bf16[160,2816]{1,0:T(8,128)(2,1)}, bf16[160,2816]{1,0:T(8,128)(2,1)}, u32[]{:S(2)}, u32[]{:S(2)}) %collective-permute-start.10) | collective-permute-done | bytes 901152 | tf_op jit(solution)/shard_map/ppermute | solution.py:89
  78.7 3.5 all-to-all-start
  86.3 4.4 shard_map.239
  90.7 14.4 %collective-permute-done.14.refs_1_ = bf16[160,2816]{1,0:T(8,128)(2,1)} collective-permute-done((bf16[160,2816]{1,0:T(8,128)(2,1)}, bf16[160,2816]{1,0:T(8,128)(2,1)}, u32[]{:S(2)}, u32[]{:S(2)}) %collective-permute-start.14) | collective-permute-done | bytes 901152 | tf_op jit(solution)/shard_map/ppermute | solution.py:80
  105.2 8.3 %all-to-all-done.own = bf16[4,160,960]{2,1,0:T(8,128)(2,1)S(1)} async-done(((bf16[4,160,960]{2,1,0:T(8,128)(2,1)}), bf16[4,160,960]{2,1,0:T(8,128)(2,1)S(1)}, u32[]{:S(2)}, u32[]{:S(2)}) %all-to-all-start) | async-done | bytes 1228832 | tf_op jit(solution)/shard_map/all_to_all | solution.py:93
  113.5 4.3 all-to-all-start.1
  117.9 4.5 shard_map.240
  122.5 3.2 copy-done.2
  125.7 3.2 shard_map.241.q_ref
  131.0 3.5 collective-permute-done.18
  135.7 3.6 shard_map.243
  141.1 7.6 %all-to-all-done.1.own = bf16[4,160,960]{2,1,0:T(8,128)(2,1)} async-done(((bf16[4,160,960]{2,1,0:T(8,128)(2,1)}), bf16[4,160,960]{2,1,0:T(8,128)(2,1)}, u32[]{:S(2)}, u32[]{:S(2)}) %all-to-all-start.1) | async-done | bytes 1228832 | tf_op jit(solution)/shard_map/all_to_all | solution.py:93
  148.7 4.8 all-to-all-start.2
  153.6 5.4 collective-permute-done.15.side
  160.6 12.4 %collective-permute-done.22.got_ref = bf16[96,2560]{1,0:T(8,128)(2,1)S(1)} collective-permute-done((bf16[96,2560]{1,0:T(8,128)(2,1)}, bf16[96,2560]{1,0:T(8,128)(2,1)S(1)}, u32[]{:S(2)}, u32[]{:S(2)}) %collective-permute-start.22) | collective-permute-done | bytes 491552 | tf_op jit(solution)/shard_map/ppermute | solution.py:86
  180.6 2.8 shard_map.244
  185.8 3.4 collective-permute-done.23.other_ref.refs_1_
  189.2 16.3 %all-to-all-done.2.own = bf16[4,160,960]{2,1,0:T(8,128)(2,1)} async-done(((bf16[4,160,960]{2,1,0:T(8,128)(2,1)}), bf16[4,160,960]{2,1,0:T(8,128)(2,1)}, u32[]{:S(2)}, u32[]{:S(2)}) %all-to-all-start.2) | async-done | bytes 1228832 | tf_op jit(solution)/shard_map/all_to_all | solution.py:93
  208.2 14.1 %collective-permute-done.30.dyo_ref.refs_4_ = bf16[96,2560]{1,0:T(8,128)(2,1)} collective-permute-done((bf16[96,2560]{1,0:T(8,128)(2,1)}, bf16[96,2560]{1,0:T(8,128)(2,1)}, u32[]{:S(2)}, u32[]{:S(2)}) %collective-permute-start.30) | collective-permute-done | bytes 491552 | tf_op jit(solution)/shard_map/ppermute | solution.py:89
  223.4 3.5 shard_map.246
  234.2 2.9 collective-permute-done.27.side
  244.6 3.7 shard_map.247
  248.3 10.8 %shard_map.248 = (bf16[192,960]{1,0:T(8,128)(2,1)S(1)}, bf16[192,960]{1,0:T(8,128)(2,1)S(1)}, bf16[192,960]{1,0:T(8,128)(2,1)S(1)}, bf16[2,96,2560]{2,1,0:T(8,12...) custom-call(bf16[2560,960]{1,0:T(8,128)(2,1)S(1)} %bitcast.72, bf16[2560,960]{1,0:T(8,128)(2,1)S(1)} %bitcast.76, ...), custom_call_target="tpu_custom_call" | custom-call | flops 383333344 | bytes 1230000 | tf_op jit(solution)/shard_map/pallas_call | solution.py:521
  260.0 3.3 collective-permute-done.34.own_ref.refs_6_
  265.4 9.9 %shard_map.249 = (bf16[192,960]{1,0:T(8,128)(2,1)S(1)}, bf16[192,960]{1,0:T(8,128)(2,1)S(1)}, bf16[192,960]{1,0:T(8,128)(2,1)S(1)}, bf16[2,96,2560]{2,1,0:T(8,12...) custom-call(bf16[2560,960]{1,0:T(8,128)(2,1)S(1)} %bitcast.73, bf16[2560,960]{1,0:T(8,128)(2,1)S(1)} %bitcast.77, ...), custom_call_target="tpu_custom_call" | custom-call | flops 383333344 | bytes 1230000 | tf_op jit(solution)/shard_map/pallas_call | solution.py:521
  275.3 9.9 %shard_map.250 = (bf16[192,960]{1,0:T(8,128)(2,1)S(1)}, bf16[192,960]{1,0:T(8,128)(2,1)S(1)}, bf16[192,960]{1,0:T(8,128)(2,1)S(1)}, bf16[2,96,2560]{2,1,0:T(8,12...) custom-call(bf16[2560,960]{1,0:T(8,128)(2,1)S(1)} %bitcast.74, bf16[2560,960]{1,0:T(8,128)(2,1)S(1)} %bitcast.78, ...), custom_call_target="tpu_custom_call" | custom-call | flops 383333344 | bytes 1230000 | tf_op jit(solution)/shard_map/pallas_call | solution.py:521
  287.5 10.0 %shard_map.251 = (bf16[192,960]{1,0:T(8,128)(2,1)S(1)}, bf16[192,960]{1,0:T(8,128)(2,1)S(1)}, bf16[192,960]{1,0:T(8,128)(2,1)S(1)}, bf16[2,96,2560]{2,1,0:T(8,12...) custom-call(bf16[2560,960]{1,0:T(8,128)(2,1)S(1)} %bitcast.75, bf16[2560,960]{1,0:T(8,128)(2,1)S(1)} %bitcast.79, ...), custom_call_target="tpu_custom_call" | custom-call | flops 383333344 | bytes 1230000 | tf_op jit(solution)/shard_map/pallas_call | solution.py:521
  297.5 7.5 %shard_map.252 = (bf16[4,2,160,960]{3,2,1,0:T(8,128)(2,1)S(1)}, bf16[1,160,960]{2,1,0:T(8,128)(2,1)S(1)}, bf16[1,160,960]{2,1,0:T(8,128)(2,1)S(1)}, bf16[1,160,9...) custom-call(s32[4]{0:T(128)S(1)} %pad_add_fusion.ranks_ref, ...), custom_call_target="tpu_custom_call" | custom-call | flops 191666672 | bytes 615000 | tf_op jit(solution)/shard_map/pallas_call | solution.py:116
  305.0 4.4 collective-permute-done.40.refs_1_
  317.2 14.0 %shard_map.255 = (bf16[4,2,160,960]{3,2,1,0:T(8,128)(2,1)S(1)}, bf16[4,2,160,960]{3,2,1,0:T(8,128)(2,1)S(1)}, bf16[2,160,960]{2,1,0:T(8,128)(2,1)S(1)}, bf16[2,1...) custom-call(s32[4]{0:T(128)S(1)} %pad_add_fusion.ranks_ref, ...), custom_call_target="tpu_custom_call" | custom-call | flops 383333344 | bytes 1230000 | tf_op jit(solution)/shard_map/pallas_call | solution.py:116
  342.6 17.0 %collective-permute-done.56.refs_2_ = bf16[2,96,2560]{2,1,0:T(8,128)(2,1)S(1)} collective-permute-done((bf16[2,96,2560]{2,1,0:T(8,128)(2,1)S(1)}, bf16[2,96,2560]{2,1,0:T(8,128)(2,1)S(1)}, u32[]{:S(2)}, u32[]{:S(2)}) %collective-permute-start.56) | collective-permute-done | bytes 983072 | tf_op jit(solution)/shard_map/ppermute | solution.py:89
  362.8 3.8 collective-permute-done.59.refs_0_
  370.7 4.9 all-to-all-start.3
  379.6 3.1 shard_map.261
  383.8 4.6 collective-permute-done.58.held_ref
  388.4 3.0 shard_map.259
  399.2 5.2 collective-permute-done.65
  412.9 4.2 shard_map.265
  425.6 4.7 all-to-all-start.4
  438.3 2.9 shard_map.266
  446.6 6.7 %shard_map.268 = (bf16[4,2,160,1536]{3,2,1,0:T(8,128)(2,1)S(1)}, bf16[2,160,1536]{2,1,0:T(8,128)(2,1)}, bf16[2,160,1536]{2,1,0:T(8,128)(2,1)}, bf16[2,160,1536]{2,1,0:T(8,128)(2,1)}, bf16[2,160,1536]{2,1,0:T(8,128)(2,1)}) custom-call(s32[4]{0:T(128)S(1)} %pad_add_fusion.ranks_ref, bf16[192,2560]{1,0:T(8,128)(2,1)S(1)} %bitcast.85, ...), custom_call_target="tpu_custom_call" | custom-call | flops 191666672 | bytes 615000 | tf_op jit(solution)/shard_map/pallas_call | solution.py:116
  455.4 4.1 shard_map.269
  465.6 5.3 all-to-all-start.5
  473.3 4.9 shard_map.270
  478.2 5.5 collective-permute-done.78.refs_1_
  498.2 6.5 %collective-permute-done.83.refs_0_ = bf16[160,1280]{1,0:T(8,128)(2,1)} collective-permute-done((bf16[160,1280]{1,0:T(8,128)(2,1)}, bf16[160,1280]{1,0:T(8,128)(2,1)}, u32[]{:S(2)}, u32[]{:S(2)}) %collective-permute-start.83) | collective-permute-done | bytes 409632 | tf_op jit(solution)/shard_map/ppermute | solution.py:89
  505.8 4.7 all-to-all-done.5.parts_ref
  517.2 3.0 shard_map.276
  520.2 5.2 collective-permute-done.85.refs_0_
  527.1 6.3 %collective-permute-done.86.refs_1_ = bf16[2,160,1536]{2,1,0:T(8,128)(2,1)S(1)} collective-permute-done((bf16[2,160,1536]{2,1,0:T(8,128)(2,1)}, bf16[2,160,1536]{2,1,0:T(8,128)(2,1)S(1)}, u32[]{:S(2)}, u32[]{:S(2)}) %collective-permute-start.86) | collective-permute-done | bytes 983072 | tf_op jit(solution)/shard_map/ppermute | solution.py:80
  535.9 4.9 copy.50
  544.9 4.5 collective-permute-done.93.refs_0_
  551.9 3.0 shard_map.284
  556.0 9.5 %collective-permute-done.94.refs_0_ = bf16[160,1536]{1,0:T(8,128)(2,1)S(1)} collective-permute-done((bf16[160,1536]{1,0:T(8,128)(2,1)S(1)}, bf16[160,1536]{1,0:T(8,128)(2,1)S(1)}, u32[]{:S(2)}, u32[]{:S(2)}) %collective-permute-start.94) | collective-permute-done | bytes 491552 | tf_op jit(solution)/shard_map/ppermute | solution.py:89
  567.5 6.8 %collective-permute-done.92.refs_0_ = bf16[160,1280]{1,0:T(8,128)(2,1)S(1)} collective-permute-done((bf16[160,1280]{1,0:T(8,128)(2,1)S(1)}, bf16[160,1280]{1,0:T(8,128)(2,1)S(1)}, u32[]{:S(2)}, u32[]{:S(2)}) %collective-permute-start.92) | collective-permute-done | bytes 409632 | tf_op jit(solution)/shard_map/ppermute | solution.py:89
  575.2 5.9 %collective-permute-done.95.refs_0_ = bf16[160,1536]{1,0:T(8,128)(2,1)S(1)} collective-permute-done((bf16[160,1536]{1,0:T(8,128)(2,1)S(1)}, bf16[160,1536]{1,0:T(8,128)(2,1)S(1)}, u32[]{:S(2)}, u32[]{:S(2)}) %collective-permute-start.95) | collective-permute-done | bytes 491552 | tf_op jit(solution)/shard_map/ppermute | solution.py:89
  583.4 3.3 collective-permute-done.96
  (473 shorter events, 192.2 us)
Async XLA Ops:
  2.8 25.2 %collective-permute-start = (bf16[160,2816]{1,0:T(8,128)(2,1)S(1)}, bf16[160,2816]{1,0:T(8,128)(2,1)}, u32[]{:S(2)}, u32[]{:S(2)}) collective-permute-start(bf16[160,2816]{1,0:T(8,128)(2,1)S(1)} %pad_maximum_fusion.refs_0_), channel_id=1, source_target_pairs={{0,8},{2,10},{4,12},{6,14},{8,16},{10,18},{12,20},{14,22},{16,24},... | collective-permute-start | bytes 2703368 | tf_op jit(solution)/shard_map/ppermute | solution.py:89
  5.8 22.1 %collective-permute-start.1 = (bf16[160,2816]{1,0:T(8,128)(2,1)S(1)}, bf16[160,2816]{1,0:T(8,128)(2,1)}, u32[]{:S(2)}, u32[]{:S(2)}) collective-permute-start(bf16[160,2816]{1,0:T(8,128)(2,1)S(1)} %pad_maximum_fusion.refs_0_), channel_id=1, source_target_pairs={{0,4},{2,6},{4,0},{6,2},{8,12},{10,14},{12,8},{14,10},{16,20},{18,... | collective-permute-start | bytes 2703368 | tf_op jit(solution)/shard_map/ppermute | solution.py:80
  7.4 24.2 %collective-permute-start.2 = (bf16[160,2816]{1,0:T(8,128)(2,1)S(1)}, bf16[160,2816]{1,0:T(8,128)(2,1)S(1)}, u32[]{:S(2)}, u32[]{:S(2)}) collective-permute-start(bf16[160,2816]{1,0:T(8,128)(2,1)S(1)} %pad_maximum_fusion.refs_0_), channel_id=1, source_target_pairs={{0,2},{2,0},{4,6},{6,4},{8,10},{10,8},{12,14},{14,12},{16,18},{18,... | collective-permute-start | bytes 2703368 | tf_op jit(solution)/shard_map/ppermute | solution.py:83
  28.0 26.1 %collective-permute-start.4 = (bf16[160,2816]{1,0:T(8,128)(2,1)}, bf16[160,2816]{1,0:T(8,128)(2,1)}, u32[]{:S(2)}, u32[]{:S(2)}) collective-permute-start(bf16[160,2816]{1,0:T(8,128)(2,1)} %collective-permute-done.refs_0_), channel_id=1, source_target_pairs={{0,2},{2,0},{4,6},{6,4},{8,10},{10,8},{12,14},{14,12},{16,18},{18,... | collective-permute-start | bytes 2703368 | tf_op jit(solution)/shard_map/ppermute | solution.py:83
  28.0 26.1 %collective-permute-start.6 = (bf16[160,2816]{1,0:T(8,128)(2,1)}, bf16[160,2816]{1,0:T(8,128)(2,1)}, u32[]{:S(2)}, u32[]{:S(2)}) collective-permute-start(bf16[160,2816]{1,0:T(8,128)(2,1)} %collective-permute-done.refs_0_), channel_id=1, source_target_pairs={{0,8},{2,10},{4,12},{6,14},{8,16},{10,18},{12,20},{14,22},{16,24},... | collective-permute-start | bytes 2703368 | tf_op jit(solution)/shard_map/ppermute | solution.py:89
  29.0 25.1 %collective-permute-start.7 = (bf16[160,2816]{1,0:T(8,128)(2,1)}, bf16[160,2816]{1,0:T(8,128)(2,1)}, u32[]{:S(2)}, u32[]{:S(2)}) collective-permute-start(bf16[160,2816]{1,0:T(8,128)(2,1)} %collective-permute-done.refs_0_), channel_id=1, source_target_pairs={{0,4},{2,6},{4,0},{6,2},{8,12},{10,14},{12,8},{14,10},{16,20},{18,... | collective-permute-start | bytes 2703368 | tf_op jit(solution)/shard_map/ppermute | solution.py:80
  30.5 18.2 %collective-permute-start.3 = (bf16[160,2816]{1,0:T(8,128)(2,1)}, bf16[160,2816]{1,0:T(8,128)(2,1)}, u32[]{:S(2)}, u32[]{:S(2)}) collective-permute-start(bf16[160,2816]{1,0:T(8,128)(2,1)} %collective-permute-done.1.refs_1_), channel_id=1, source_target_pairs={{0,2},{2,0},{4,6},{6,4},{8,10},{10,8},{12,14},{14,12},{16,18},{18,... | collective-permute-start | bytes 2703368 | tf_op jit(solution)/shard_map/ppermute | solution.py:83
  31.5 22.6 %collective-permute-start.5 = (bf16[96,2560]{1,0:T(8,128)(2,1)S(1)}, bf16[96,2560]{1,0:T(8,128)(2,1)}, u32[]{:S(2)}, u32[]{:S(2)}) collective-permute-start(bf16[96,2560]{1,0:T(8,128)(2,1)S(1)} %bitcast.86), channel_id=1, source_target_pairs={{0,1},{1,0},{2,3},{3,2},{4,5},{5,4},{6,7},{7,6},{8,9},{9,8},{10,11... | collective-permute-start | bytes 1474568 | tf_op jit(solution)/shard_map/ppermute | solution.py:86
  54.4 24.3 %collective-permute-start.10 = (bf16[160,2816]{1,0:T(8,128)(2,1)}, bf16[160,2816]{1,0:T(8,128)(2,1)}, u32[]{:S(2)}, u32[]{:S(2)}) collective-permute-start(bf16[160,2816]{1,0:T(8,128)(2,1)} %collective-permute-done.6.refs_0_), channel_id=1, source_target_pairs={{0,8},{2,10},{4,12},{6,14},{8,16},{10,18},{12,20},{14,22},{16,24},... | collective-permute-start | bytes 2703368 | tf_op jit(solution)/shard_map/ppermute | solution.py:89
  55.9 22.8 %collective-permute-start.11 = (bf16[160,2816]{1,0:T(8,128)(2,1)}, bf16[160,2816]{1,0:T(8,128)(2,1)}, u32[]{:S(2)}, u32[]{:S(2)}) collective-permute-start(bf16[160,2816]{1,0:T(8,128)(2,1)} %collective-permute-done.6.refs_0_), channel_id=1, source_target_pairs={{0,4},{2,6},{4,0},{6,2},{8,12},{10,14},{12,8},{14,10},{16,20},{18,... | collective-permute-start | bytes 2703368 | tf_op jit(solution)/shard_map/ppermute | solution.py:80
  78.7 34.8 %all-to-all-start = ((bf16[4,160,960]{2,1,0:T(8,128)(2,1)}), bf16[4,160,960]{2,1,0:T(8,128)(2,1)S(1)}, u32[]{:S(2)}, u32[]{:S(2)}) async-start(bf16[4,160,960]{2,1,0:T(8,128)(2,1)} %bitcast.105), calls=%async_computation | async-start | bytes 2621440 | tf_op jit(solution)/shard_map/all_to_all | solution.py:93
  82.9 22.3 %collective-permute-start.14 = (bf16[160,2816]{1,0:T(8,128)(2,1)}, bf16[160,2816]{1,0:T(8,128)(2,1)}, u32[]{:S(2)}, u32[]{:S(2)}) collective-permute-start(bf16[160,2816]{1,0:T(8,128)(2,1)} %collective-permute-done.10.refs_0_), channel_id=1, source_target_pairs={{0,4},{2,6},{4,0},{6,2},{8,12},{10,14},{12,8},{14,10},{16,20},{18,... | collective-permute-start | bytes 2703368 | tf_op jit(solution)/shard_map/ppermute | solution.py:80
  113.5 35.2 %all-to-all-start.1 = ((bf16[4,160,960]{2,1,0:T(8,128)(2,1)}), bf16[4,160,960]{2,1,0:T(8,128)(2,1)}, u32[]{:S(2)}, u32[]{:S(2)}) async-start(bf16[4,160,960]{2,1,0:T(8,128)(2,1)} %bitcast.107), calls=%async_computation.1 | async-start | bytes 2621440 | tf_op jit(solution)/shard_map/all_to_all | solution.py:93
  129.0 29.9 %collective-permute-start.15 = (bf16[4,160,960]{2,1,0:T(8,128)(2,1)S(1)}, bf16[4,160,960]{2,1,0:T(8,128)(2,1)}, u32[]{:S(2)}, u32[]{:S(2)}) collective-permute-start(bf16[4,160,960]{2,1,0:T(8,128)(2,1)S(1)} %all-to-all-done.own), channel_id=1, source_target_pairs={{0,4},{2,6},{4,0},{6,2},{8,12},{10,14},{12,8},{14,10},{16,20},{18,... | collective-permute-start | bytes 3686408 | tf_op jit(solution)/shard_map/ppermute | solution.py:80
  148.7 56.7 %all-to-all-start.2 = ((bf16[4,160,960]{2,1,0:T(8,128)(2,1)}), bf16[4,160,960]{2,1,0:T(8,128)(2,1)}, u32[]{:S(2)}, u32[]{:S(2)}) async-start(bf16[4,160,960]{2,1,0:T(8,128)(2,1)} %bitcast.106), calls=%async_computation.2 | async-start | bytes 2621440 | tf_op jit(solution)/shard_map/all_to_all | solution.py:93
  153.5 25.8 %collective-permute-start.16 = (bf16[4,160,960]{2,1,0:T(8,128)(2,1)S(1)}, bf16[4,160,960]{2,1,0:T(8,128)(2,1)S(1)}, u32[]{:S(2)}, u32[]{:S(2)}) collective-permute-start(bf16[4,160,960]{2,1,0:T(8,128)(2,1)S(1)} %all-to-all-done.own), channel_id=1, source_target_pairs={{0,2},{2,0},{4,6},{6,4},{8,10},{10,8},{12,14},{14,12},{16,18},{18,... | collective-permute-start | bytes 3686408 | tf_op jit(solution)/shard_map/ppermute | solution.py:83
  158.9 21.7 %collective-permute-start.19 = (bf16[4,160,960]{2,1,0:T(8,128)(2,1)}, bf16[4,160,960]{2,1,0:T(8,128)(2,1)S(1)}, u32[]{:S(2)}, u32[]{:S(2)}) collective-permute-start(bf16[4,160,960]{2,1,0:T(8,128)(2,1)} %collective-permute-done.15.side), channel_id=1, source_target_pairs={{0,2},{2,0},{4,6},{6,4},{8,10},{10,8},{12,14},{14,12},{16,18},{18,... | collective-permute-start | bytes 3686408 | tf_op jit(solution)/shard_map/ppermute | solution.py:83
  158.9 46.5 %collective-permute-start.20 = (bf16[4,160,960]{2,1,0:T(8,128)(2,1)}, bf16[4,160,960]{2,1,0:T(8,128)(2,1)}, u32[]{:S(2)}, u32[]{:S(2)}) collective-permute-start(bf16[4,160,960]{2,1,0:T(8,128)(2,1)} %all-to-all-done.1.own), channel_id=1, source_target_pairs={{0,4},{2,6},{4,0},{6,2},{8,12},{10,14},{12,8},{14,10},{16,20},{18,... | collective-permute-start | bytes 3686408 | tf_op jit(solution)/shard_map/ppermute | solution.py:80
  159.5 13.6 %collective-permute-start.22 = (bf16[96,2560]{1,0:T(8,128)(2,1)}, bf16[96,2560]{1,0:T(8,128)(2,1)S(1)}, u32[]{:S(2)}, u32[]{:S(2)}) collective-permute-start(bf16[96,2560]{1,0:T(8,128)(2,1)} %copy-done.83), channel_id=1, source_target_pairs={{0,1},{1,0},{2,3},{3,2},{4,5},{5,4},{6,7},{7,6},{8,9},{9,8},{10,11... | collective-permute-start | bytes 1474568 | tf_op jit(solution)/shard_map/ppermute | solution.py:86
  177.4 28.0 %collective-permute-start.25 = (bf16[96,2560]{1,0:T(8,128)(2,1)S(1)}, bf16[96,2560]{1,0:T(8,128)(2,1)}, u32[]{:S(2)}, u32[]{:S(2)}) collective-permute-start(bf16[96,2560]{1,0:T(8,128)(2,1)S(1)} %bitcast.87), channel_id=1, source_target_pairs={{0,8},{2,10},{4,12},{6,14},{8,16},{10,18},{12,20},{14,22},{16,24},... | collective-permute-start | bytes 1474568 | tf_op jit(solution)/shard_map/ppermute | solution.py:89
  179.3 26.2 %collective-permute-start.24 = (bf16[96,2560]{1,0:T(8,128)(2,1)}, bf16[96,2560]{1,0:T(8,128)(2,1)}, u32[]{:S(2)}, u32[]{:S(2)}) collective-permute-start(bf16[96,2560]{1,0:T(8,128)(2,1)} %get-tuple-element.472.own_ref.refs_0_), channel_id=1, source_target_pairs={{0,8},{2,10},{4,12},{6,14},{8,16},{10,18},{12,20},{14,22},{16,24},... | collective-permute-start | bytes 1474568 | tf_op jit(solution)/shard_map/ppermute | solution.py:89
  180.6 26.5 %collective-permute-start.21 = (bf16[4,160,960]{2,1,0:T(8,128)(2,1)}, bf16[4,160,960]{2,1,0:T(8,128)(2,1)}, u32[]{:S(2)}, u32[]{:S(2)}) collective-permute-start(bf16[4,160,960]{2,1,0:T(8,128)(2,1)} %all-to-all-done.1.own), channel_id=1, source_target_pairs={{0,2},{2,0},{4,6},{6,4},{8,10},{10,8},{12,14},{14,12},{16,18},{18,... | collective-permute-start | bytes 3686408 | tf_op jit(solution)/shard_map/ppermute | solution.py:83
  205.5 17.9 %collective-permute-start.26 = (bf16[4,160,960]{2,1,0:T(8,128)(2,1)}, bf16[4,160,960]{2,1,0:T(8,128)(2,1)S(1)}, u32[]{:S(2)}, u32[]{:S(2)}) collective-permute-start(bf16[4,160,960]{2,1,0:T(8,128)(2,1)} %collective-permute-done.20.side), channel_id=1, source_target_pairs={{0,2},{2,0},{4,6},{6,4},{8,10},{10,8},{12,14},{14,12},{16,18},{18,... | collective-permute-start | bytes 3686408 | tf_op jit(solution)/shard_map/ppermute | solution.py:83
  205.6 31.5 %collective-permute-start.27 = (bf16[4,160,960]{2,1,0:T(8,128)(2,1)}, bf16[4,160,960]{2,1,0:T(8,128)(2,1)}, u32[]{:S(2)}, u32[]{:S(2)}) collective-permute-start(bf16[4,160,960]{2,1,0:T(8,128)(2,1)} %all-to-all-done.2.own), channel_id=1, source_target_pairs={{0,4},{2,6},{4,0},{6,2},{8,12},{10,14},{12,8},{14,10},{16,20},{18,... | collective-permute-start | bytes 3686408 | tf_op jit(solution)/shard_map/ppermute | solution.py:80
  206.1 16.2 %collective-permute-start.30 = (bf16[96,2560]{1,0:T(8,128)(2,1)}, bf16[96,2560]{1,0:T(8,128)(2,1)}, u32[]{:S(2)}, u32[]{:S(2)}) collective-permute-start(bf16[96,2560]{1,0:T(8,128)(2,1)} %collective-permute-done.25.dyo_ref.refs_2_), channel_id=1, source_target_pairs={{0,8},{2,10},{4,12},{6,14},{8,16},{10,18},{12,20},{14,22},{16,24},... | collective-permute-start | bytes 1474568 | tf_op jit(solution)/shard_map/ppermute | solution.py:89
  206.1 25.8 %collective-permute-start.29 = (bf16[96,2560]{1,0:T(8,128)(2,1)}, bf16[96,2560]{1,0:T(8,128)(2,1)S(1)}, u32[]{:S(2)}, u32[]{:S(2)}) collective-permute-start(bf16[96,2560]{1,0:T(8,128)(2,1)} %collective-permute-done.24.own_ref.refs_2_), channel_id=1, source_target_pairs={{0,8},{2,10},{4,12},{6,14},{8,16},{10,18},{12,20},{14,22},{16,24},... | collective-permute-start | bytes 1474568 | tf_op jit(solution)/shard_map/ppermute | solution.py:89
  207.1 24.9 %collective-permute-start.32 = (bf16[96,2560]{1,0:T(8,128)(2,1)}, bf16[96,2560]{1,0:T(8,128)(2,1)S(1)}, u32[]{:S(2)}, u32[]{:S(2)}) collective-permute-start(bf16[96,2560]{1,0:T(8,128)(2,1)} %collective-permute-done.25.dyo_ref.refs_2_), channel_id=1, source_target_pairs={{0,1},{1,0},{2,3},{3,2},{4,5},{5,4},{6,7},{7,6},{8,9},{9,8},{10,11... | collective-permute-start | bytes 1474568 | tf_op jit(solution)/shard_map/ppermute | solution.py:86
  223.4 15.2 %collective-permute-start.28 = (bf16[4,160,960]{2,1,0:T(8,128)(2,1)}, bf16[4,160,960]{2,1,0:T(8,128)(2,1)S(1)}, u32[]{:S(2)}, u32[]{:S(2)}) collective-permute-start(bf16[4,160,960]{2,1,0:T(8,128)(2,1)} %all-to-all-done.2.own), channel_id=1, source_target_pairs={{0,2},{2,0},{4,6},{6,4},{8,10},{10,8},{12,14},{14,12},{16,18},{18,... | collective-permute-start | bytes 3686408 | tf_op jit(solution)/shard_map/ppermute | solution.py:83
  237.1 23.0 %collective-permute-start.35 = (bf16[96,2560]{1,0:T(8,128)(2,1)}, bf16[96,2560]{1,0:T(8,128)(2,1)}, u32[]{:S(2)}, u32[]{:S(2)}) collective-permute-start(bf16[96,2560]{1,0:T(8,128)(2,1)} %collective-permute-done.30.dyo_ref.refs_4_), channel_id=1, source_target_pairs={{0,8},{2,10},{4,12},{6,14},{8,16},{10,18},{12,20},{14,22},{16,24},... | collective-permute-start | bytes 1474568 | tf_op jit(solution)/shard_map/ppermute | solution.py:89
  237.1 26.3 %collective-permute-start.34 = (bf16[96,2560]{1,0:T(8,128)(2,1)S(1)}, bf16[96,2560]{1,0:T(8,128)(2,1)}, u32[]{:S(2)}, u32[]{:S(2)}) collective-permute-start(bf16[96,2560]{1,0:T(8,128)(2,1)S(1)} %collective-permute-done.29.own_ref.refs_4_), channel_id=1, source_target_pairs={{0,8},{2,10},{4,12},{6,14},{8,16},{10,18},{12,20},{14,22},{16,24},... | collective-permute-start | bytes 1474568 | tf_op jit(solution)/shard_map/ppermute | solution.py:89
  238.1 25.3 %collective-permute-start.37 = (bf16[96,2560]{1,0:T(8,128)(2,1)}, bf16[96,2560]{1,0:T(8,128)(2,1)}, u32[]{:S(2)}, u32[]{:S(2)}) collective-permute-start(bf16[96,2560]{1,0:T(8,128)(2,1)} %collective-permute-done.30.dyo_ref.refs_4_), channel_id=1, source_target_pairs={{0,1},{1,0},{2,3},{3,2},{4,5},{5,4},{6,7},{7,6},{8,9},{9,8},{10,11... | collective-permute-start | bytes 1474568 | tf_op jit(solution)/shard_map/ppermute | solution.py:86
  239.7 23.7 %collective-permute-start.36 = (bf16[96,2560]{1,0:T(8,128)(2,1)S(1)}, bf16[96,2560]{1,0:T(8,128)(2,1)}, u32[]{:S(2)}, u32[]{:S(2)}) collective-permute-start(bf16[96,2560]{1,0:T(8,128)(2,1)S(1)} %collective-permute-done.29.own_ref.refs_4_), channel_id=1, source_target_pairs={{0,1},{1,0},{2,3},{3,2},{4,5},{5,4},{6,7},{7,6},{8,9},{9,8},{10,11... | collective-permute-start | bytes 1474568 | tf_op jit(solution)/shard_map/ppermute | solution.py:86
  263.4 21.9 %collective-permute-start.39 = (bf16[96,2560]{1,0:T(8,128)(2,1)}, bf16[96,2560]{1,0:T(8,128)(2,1)S(1)}, u32[]{:S(2)}, u32[]{:S(2)}) collective-permute-start(bf16[96,2560]{1,0:T(8,128)(2,1)} %collective-permute-done.35.dyo_ref.refs_6_), channel_id=1, source_target_pairs={{0,1},{1,0},{2,3},{3,2},{4,5},{5,4},{6,7},{7,6},{8,9},{9,8},{10,11... | collective-permute-start | bytes 1474568 | tf_op jit(solution)/shard_map/ppermute | solution.py:86
  263.9 23.1 %collective-permute-start.38 = (bf16[96,2560]{1,0:T(8,128)(2,1)}, bf16[96,2560]{1,0:T(8,128)(2,1)S(1)}, u32[]{:S(2)}, u32[]{:S(2)}) collective-permute-start(bf16[96,2560]{1,0:T(8,128)(2,1)} %collective-permute-done.34.own_ref.refs_6_), channel_id=1, source_target_pairs={{0,1},{1,0},{2,3},{3,2},{4,5},{5,4},{6,7},{7,6},{8,9},{9,8},{10,11... | collective-permute-start | bytes 1474568 | tf_op jit(solution)/shard_map/ppermute | solution.py:86
  287.0 22.5 %collective-permute-start.40 = (bf16[2,96,2560]{2,1,0:T(8,128)(2,1)S(1)}, bf16[2,96,2560]{2,1,0:T(8,128)(2,1)S(1)}, u32[]{:S(2)}, u32[]{:S(2)}) collective-permute-start(bf16[2,96,2560]{2,1,0:T(8,128)(2,1)S(1)} %get-tuple-element.449), channel_id=1, source_target_pairs={{0,1},{1,0},{2,3},{3,2},{4,5},{5,4},{6,7},{7,6},{8,9},{9,8},{10,11... | collective-permute-start | bytes 2949128 | tf_op jit(solution)/shard_map/ppermute | solution.py:86
  309.7 23.4 %collective-permute-start.50 = (bf16[2,96,2560]{2,1,0:T(8,128)(2,1)S(1)}, bf16[2,96,2560]{2,1,0:T(8,128)(2,1)S(1)}, u32[]{:S(2)}, u32[]{:S(2)}) collective-permute-start(bf16[2,96,2560]{2,1,0:T(8,128)(2,1)S(1)} %shard_map.253), channel_id=1, source_target_pairs={{0,8},{2,10},{4,12},{6,14},{8,16},{10,18},{12,20},{14,22},{16,24},... | collective-permute-start | bytes 2949128 | tf_op jit(solution)/shard_map/ppermute | solution.py:89
  309.7 23.4 %collective-permute-start.49 = (bf16[2,96,2560]{2,1,0:T(8,128)(2,1)S(1)}, bf16[2,96,2560]{2,1,0:T(8,128)(2,1)S(1)}, u32[]{:S(2)}, u32[]{:S(2)}) collective-permute-start(bf16[2,96,2560]{2,1,0:T(8,128)(2,1)S(1)} %get-tuple-element.481), channel_id=1, source_target_pairs={{0,1},{1,0},{2,3},{3,2},{4,5},{5,4},{6,7},{7,6},{8,9},{9,8},{10,11... | collective-permute-start | bytes 2949128 | tf_op jit(solution)/shard_map/ppermute | solution.py:86
  334.0 25.5 %collective-permute-start.56 = (bf16[2,96,2560]{2,1,0:T(8,128)(2,1)S(1)}, bf16[2,96,2560]{2,1,0:T(8,128)(2,1)S(1)}, u32[]{:S(2)}, u32[]{:S(2)}) collective-permute-start(bf16[2,96,2560]{2,1,0:T(8,128)(2,1)S(1)} %shard_map.256), channel_id=1, source_target_pairs={{0,8},{2,10},{4,12},{6,14},{8,16},{10,18},{12,20},{14,22},{16,24},... | collective-permute-start | bytes 2949128 | tf_op jit(solution)/shard_map/ppermute | solution.py:89
  334.8 24.7 %collective-permute-start.55 = (bf16[2,96,2560]{2,1,0:T(8,128)(2,1)S(1)}, bf16[2,96,2560]{2,1,0:T(8,128)(2,1)S(1)}, u32[]{:S(2)}, u32[]{:S(2)}) collective-permute-start(bf16[2,96,2560]{2,1,0:T(8,128)(2,1)S(1)} %get-tuple-element.497), channel_id=1, source_target_pairs={{0,1},{1,0},{2,3},{3,2},{4,5},{5,4},{6,7},{7,6},{8,9},{9,8},{10,11... | collective-permute-start | bytes 2949128 | tf_op jit(solution)/shard_map/ppermute | solution.py:86
  336.3 30.3 %collective-permute-start.59 = (bf16[4,160,960]{2,1,0:T(8,128)(2,1)S(1)}, bf16[4,160,960]{2,1,0:T(8,128)(2,1)S(1)}, u32[]{:S(2)}, u32[]{:S(2)}) collective-permute-start(bf16[4,160,960]{2,1,0:T(8,128)(2,1)S(1)} %get-tuple-element.506), channel_id=1, source_target_pairs={{0,4},{2,6},{4,0},{6,2},{8,12},{10,14},{12,8},{14,10},{16,20},{18,... | collective-permute-start | bytes 3686408 | tf_op jit(solution)/shard_map/ppermute | solution.py:80
  361.5 26.9 %collective-permute-start.58 = (bf16[2,96,2560]{2,1,0:T(8,128)(2,1)}, bf16[2,96,2560]{2,1,0:T(8,128)(2,1)}, u32[]{:S(2)}, u32[]{:S(2)}) collective-permute-start(bf16[2,96,2560]{2,1,0:T(8,128)(2,1)} %shard_map.258), channel_id=1, source_target_pairs={{0,8},{2,10},{4,12},{6,14},{8,16},{10,18},{12,20},{14,22},{16,24},... | collective-permute-start | bytes 2949128 | tf_op jit(solution)/shard_map/ppermute | solution.py:89
  361.5 26.9 %collective-permute-start.57 = (bf16[2,96,2560]{2,1,0:T(8,128)(2,1)}, bf16[2,96,2560]{2,1,0:T(8,128)(2,1)}, u32[]{:S(2)}, u32[]{:S(2)}) collective-permute-start(bf16[2,96,2560]{2,1,0:T(8,128)(2,1)} %get-tuple-element.501), channel_id=1, source_target_pairs={{0,1},{1,0},{2,3},{3,2},{4,5},{5,4},{6,7},{7,6},{8,9},{9,8},{10,11... | collective-permute-start | bytes 2949128 | tf_op jit(solution)/shard_map/ppermute | solution.py:86
  366.6 29.7 %collective-permute-start.64 = (bf16[4,160,960]{2,1,0:T(8,128)(2,1)}, bf16[4,160,960]{2,1,0:T(8,128)(2,1)}, u32[]{:S(2)}, u32[]{:S(2)}) collective-permute-start(bf16[4,160,960]{2,1,0:T(8,128)(2,1)} %get-tuple-element.528), channel_id=1, source_target_pairs={{0,4},{2,6},{4,0},{6,2},{8,12},{10,14},{12,8},{14,10},{16,20},{18,... | collective-permute-start | bytes 3686408 | tf_op jit(solution)/shard_map/ppermute | solution.py:80
  370.7 54.8 %all-to-all-start.3 = ((bf16[4,160,960]{2,1,0:T(8,128)(2,1)}), bf16[4,160,960]{2,1,0:T(8,128)(2,1)S(1)}, u32[]{:S(2)}, u32[]{:S(2)}) async-start(bf16[4,160,960]{2,1,0:T(8,128)(2,1)} %copy-done.11), calls=%async_computation.3 | async-start | bytes 2621440 | tf_op jit(solution)/shard_map/all_to_all | solution.py:93
  396.3 14.9 %collective-permute-start.66 = (bf16[2,160,960]{2,1,0:T(8,128)(2,1)S(1)}, bf16[2,160,960]{2,1,0:T(8,128)(2,1)S(1)}, u32[]{:S(2)}, u32[]{:S(2)}) collective-permute-start(bf16[2,160,960]{2,1,0:T(8,128)(2,1)S(1)} %get-tuple-element.538), channel_id=1, source_target_pairs={{0,4},{2,6},{4,0},{6,2},{8,12},{10,14},{12,8},{14,10},{16,20},{18,... | collective-permute-start | bytes 1843208 | tf_op jit(solution)/shard_map/ppermute | solution.py:80
  411.2 13.5 %collective-permute-start.68 = (bf16[2,160,960]{2,1,0:T(8,128)(2,1)S(1)}, bf16[2,160,960]{2,1,0:T(8,128)(2,1)S(1)}, u32[]{:S(2)}, u32[]{:S(2)}) collective-permute-start(bf16[2,160,960]{2,1,0:T(8,128)(2,1)S(1)} %get-tuple-element.545), channel_id=1, source_target_pairs={{0,4},{2,6},{4,0},{6,2},{8,12},{10,14},{12,8},{14,10},{16,20},{18,... | collective-permute-start | bytes 1843208 | tf_op jit(solution)/shard_map/ppermute | solution.py:80
  425.6 36.6 %all-to-all-start.4 = ((bf16[4,160,960]{2,1,0:T(8,128)(2,1)}), bf16[4,160,960]{2,1,0:T(8,128)(2,1)}, u32[]{:S(2)}, u32[]{:S(2)}) async-start(bf16[4,160,960]{2,1,0:T(8,128)(2,1)} %copy-done.10), calls=%async_computation.4 | async-start | bytes 2621440 | tf_op jit(solution)/shard_map/all_to_all | solution.py:93
  443.3 20.6 %collective-permute-start.73 = (bf16[2,160,1280]{2,1,0:T(8,128)(2,1)}, bf16[2,160,1280]{2,1,0:T(8,128)(2,1)}, u32[]{:S(2)}, u32[]{:S(2)}) collective-permute-start(bf16[2,160,1280]{2,1,0:T(8,128)(2,1)} %get-tuple-element.573), channel_id=1, source_target_pairs={{0,4},{2,6},{4,0},{6,2},{8,12},{10,14},{12,8},{14,10},{16,20},{18,... | collective-permute-start | bytes 2457608 | tf_op jit(solution)/shard_map/ppermute | solution.py:80
  463.9 19.8 %collective-permute-start.78 = (bf16[2,160,1280]{2,1,0:T(8,128)(2,1)}, bf16[2,160,1280]{2,1,0:T(8,128)(2,1)}, u32[]{:S(2)}, u32[]{:S(2)}) collective-permute-start(bf16[2,160,1280]{2,1,0:T(8,128)(2,1)} %copy-done.77), channel_id=1, source_target_pairs={{0,4},{2,6},{4,0},{6,2},{8,12},{10,14},{12,8},{14,10},{16,20},{18,... | collective-permute-start | bytes 2457608 | tf_op jit(solution)/shard_map/ppermute | solution.py:80
  464.4 22.5 %collective-permute-start.79 = (bf16[96,2560]{1,0:T(8,128)(2,1)}, bf16[96,2560]{1,0:T(8,128)(2,1)}, u32[]{:S(2)}, u32[]{:S(2)}) collective-permute-start(bf16[96,2560]{1,0:T(8,128)(2,1)} %copy-done.82), channel_id=1, source_target_pairs={{0,1},{1,0},{2,3},{3,2},{4,5},{5,4},{6,7},{7,6},{8,9},{9,8},{10,11... | collective-permute-start | bytes 1474568 | tf_op jit(solution)/shard_map/ppermute | solution.py:86
  465.6 45.0 %all-to-all-start.5 = ((bf16[4,160,960]{2,1,0:T(8,128)(2,1)}), bf16[4,160,960]{2,1,0:T(8,128)(2,1)}, u32[]{:S(2)}, u32[]{:S(2)}) async-start(bf16[4,160,960]{2,1,0:T(8,128)(2,1)} %shard_map.267), calls=%async_computation.5 | async-start | bytes 2621440 | tf_op jit(solution)/shard_map/all_to_all | solution.py:93
  483.7 26.9 %collective-permute-start.84 = (bf16[2,160,1536]{2,1,0:T(8,128)(2,1)}, bf16[2,160,1536]{2,1,0:T(8,128)(2,1)}, u32[]{:S(2)}, u32[]{:S(2)}) collective-permute-start(bf16[2,160,1536]{2,1,0:T(8,128)(2,1)} %get-tuple-element.615), channel_id=1, source_target_pairs={{0,4},{2,6},{4,0},{6,2},{8,12},{10,14},{12,8},{14,10},{16,20},{18,... | collective-permute-start | bytes 2949128 | tf_op jit(solution)/shard_map/ppermute | solution.py:80
  510.5 22.9 %collective-permute-start.86 = (bf16[2,160,1536]{2,1,0:T(8,128)(2,1)}, bf16[2,160,1536]{2,1,0:T(8,128)(2,1)S(1)}, u32[]{:S(2)}, u32[]{:S(2)}) collective-permute-start(bf16[2,160,1536]{2,1,0:T(8,128)(2,1)} %get-tuple-element.622), channel_id=1, source_target_pairs={{0,4},{2,6},{4,0},{6,2},{8,12},{10,14},{12,8},{14,10},{16,20},{18,... | collective-permute-start | bytes 2949128 | tf_op jit(solution)/shard_map/ppermute | solution.py:80
  511.3 14.1 %collective-permute-start.85 = (bf16[160,1280]{1,0:T(8,128)(2,1)S(1)}, bf16[160,1280]{1,0:T(8,128)(2,1)S(1)}, u32[]{:S(2)}, u32[]{:S(2)}) collective-permute-start(bf16[160,1280]{1,0:T(8,128)(2,1)S(1)} %shard_map.275), channel_id=1, source_target_pairs={{0,8},{2,10},{4,12},{6,14},{8,16},{10,18},{12,20},{14,22},{16,24},... | collective-permute-start | bytes 1228808 | tf_op jit(solution)/shard_map/ppermute | solution.py:89
  511.4 29.4 %collective-permute-start.87 = (f32[15360]{0:T(1024)S(1)}, f32[15360]{0:T(1024)S(1)}, u32[]{:S(2)}, u32[]{:S(2)}) collective-permute-start(f32[15360]{0:T(1024)S(1)} %add.156), channel_id=1, source_target_pairs={{0,8},{2,10},{4,12},{6,14},{8,16},{10,18},{12,20},{14,22},{16,24},... | collective-permute-start | bytes 184328 | tf_op jit(solution)/shard_map/ppermute | solution.py:89
  513.7 27.1 %collective-permute-start.88 = (f32[15360]{0:T(1024)S(1)}, f32[15360]{0:T(1024)}, u32[]{:S(2)}, u32[]{:S(2)}) collective-permute-start(f32[15360]{0:T(1024)S(1)} %add.156), channel_id=1, source_target_pairs={{0,16},{2,18},{4,20},{6,22},{8,24},{10,26},{12,28},{14,30},{16,0},... | collective-permute-start | bytes 184328 | tf_op jit(solution)/shard_map/ppermute | solution.py:89
  515.7 25.7 %collective-permute-start.89 = (f32[15360]{0:T(1024)S(1)}, f32[15360]{0:T(1024)}, u32[]{:S(2)}, u32[]{:S(2)}) collective-permute-start(f32[15360]{0:T(1024)S(1)} %add.156), channel_id=1, source_target_pairs={{0,24},{2,26},{4,28},{6,30},{8,0},{10,2},{12,4},{14,6},{16,8},{18,... | collective-permute-start | bytes 184328 | tf_op jit(solution)/shard_map/ppermute | solution.py:89
  525.4 16.9 %collective-permute-start.80 = (bf16[96,2560]{1,0:T(8,128)(2,1)S(1)}, bf16[96,2560]{1,0:T(8,128)(2,1)}, u32[]{:S(2)}, u32[]{:S(2)}) collective-permute-start(bf16[96,2560]{1,0:T(8,128)(2,1)S(1)} %copy-done.71), channel_id=1, source_target_pairs={{0,1},{1,0},{2,3},{3,2},{4,5},{5,4},{6,7},{7,6},{8,9},{9,8},{10,11... | collective-permute-start | bytes 1474568 | tf_op jit(solution)/shard_map/ppermute | solution.py:86
  535.9 13.5 %collective-permute-start.93 = (bf16[160,1536]{1,0:T(8,128)(2,1)}, bf16[160,1536]{1,0:T(8,128)(2,1)S(1)}, u32[]{:S(2)}, u32[]{:S(2)}) collective-permute-start(bf16[160,1536]{1,0:T(8,128)(2,1)} %shard_map.279), channel_id=1, source_target_pairs={{0,8},{2,10},{4,12},{6,14},{8,16},{10,18},{12,20},{14,22},{16,24},... | collective-permute-start | bytes 1474568 | tf_op jit(solution)/shard_map/ppermute | solution.py:89
  542.4 13.0 %collective-permute-start.91 = (f32[15360]{0:T(1024)S(1)}, f32[15360]{0:T(1024)S(1)}, u32[]{:S(2)}, u32[]{:S(2)}) collective-permute-start(f32[15360]{0:T(1024)S(1)} %select_add_fusion), channel_id=1, source_target_pairs={{0,4},{2,6},{4,0},{6,2},{8,12},{10,14},{12,8},{14,10},{16,20},{18,... | collective-permute-start | bytes 184328 | tf_op jit(solution)/shard_map/ppermute | solution.py:80
  543.2 23.1 %collective-permute-start.90 = (bf16[96,2560]{1,0:T(8,128)(2,1)}, bf16[96,2560]{1,0:T(8,128)(2,1)S(1)}, u32[]{:S(2)}, u32[]{:S(2)}) collective-permute-start(bf16[96,2560]{1,0:T(8,128)(2,1)} %copy-done.72), channel_id=1, source_target_pairs={{0,1},{1,0},{2,3},{3,2},{4,5},{5,4},{6,7},{7,6},{8,9},{9,8},{10,11... | collective-permute-start | bytes 1474568 | tf_op jit(solution)/shard_map/ppermute | solution.py:86
  549.5 16.0 %collective-permute-start.94 = (bf16[160,1536]{1,0:T(8,128)(2,1)S(1)}, bf16[160,1536]{1,0:T(8,128)(2,1)S(1)}, u32[]{:S(2)}, u32[]{:S(2)}) collective-permute-start(bf16[160,1536]{1,0:T(8,128)(2,1)S(1)} %shard_map.280), channel_id=1, source_target_pairs={{0,8},{2,10},{4,12},{6,14},{8,16},{10,18},{12,20},{14,22},{16,24},... | collective-permute-start | bytes 1474568 | tf_op jit(solution)/shard_map/ppermute | solution.py:89
  554.9 19.4 %collective-permute-start.92 = (bf16[160,1280]{1,0:T(8,128)(2,1)S(1)}, bf16[160,1280]{1,0:T(8,128)(2,1)S(1)}, u32[]{:S(2)}, u32[]{:S(2)}) collective-permute-start(bf16[160,1280]{1,0:T(8,128)(2,1)S(1)} %shard_map.277), channel_id=1, source_target_pairs={{0,8},{2,10},{4,12},{6,14},{8,16},{10,18},{12,20},{14,22},{16,24},... | collective-permute-start | bytes 1228808 | tf_op jit(solution)/shard_map/ppermute | solution.py:89
  565.6 15.6 %collective-permute-start.95 = (bf16[160,1536]{1,0:T(8,128)(2,1)S(1)}, bf16[160,1536]{1,0:T(8,128)(2,1)S(1)}, u32[]{:S(2)}, u32[]{:S(2)}) collective-permute-start(bf16[160,1536]{1,0:T(8,128)(2,1)S(1)} %shard_map.281), channel_id=1, source_target_pairs={{0,8},{2,10},{4,12},{6,14},{8,16},{10,18},{12,20},{14,22},{16,24},... | collective-permute-start | bytes 1474568 | tf_op jit(solution)/shard_map/ppermute | solution.py:89
  (142 other events, 875.8 us)
